TPU v7x, 32 devices: a whole 2x2x4 slice. The times are simulated.
32 devices in a mesh: grp: 2 (over x), tp: 8 (over z, y), rb: 2 (over core).
Axes of the slice: x: 2, y: 2, z: 4, core: 2. Of those that a mesh axis runs over, the one named last changes fastest.
Arguments:
- peram: bfloat16 [2048, 24, 2, 1024], P(('grp', 'tp'), None, None, 'rb'), parts along dimension 0, may hold values from -1 to 1
- src_elems: bfloat16 [14, 2, 256, 256], P('grp'), parts along dimension 0, may hold values from -0.25 to 0.25
- owner_times: int32 [16, 2], P('grp'), parts along dimension 0, may hold values from 0 to 23
- diag_mom: int32 [16, 2, 2], P(('grp', 'tp')), parts along dimension 0, may hold values from 0 to 6
- diag_count: int32 [16], P(('grp', 'tp')), parts along dimension 0, may hold values from 1 to 2, as said below
Outputs:
- corr: float32 [16, 2, 2, 2], P(('grp', 'tp')), parts along dimension 0
There are 2 independent parts, one for each index of `grp`. A program takes and returns all parts, laid end to end along the dimension named above; each array names one. Nothing has to cross between parts.
Inputs may be any that keep to these rules, and one draw needn't show every extreme that they name: `diag_count`: some pair has 2 assignments.
All inputs are finite; a program needn't handle non-finite values.
Results may differ from a plain program's by a relative error of at most 0.0031.
Values may be sent and summed in bfloat16 or wider, within the bound.
No kernel may reach another device: no remote copies, remote signals or barrier semaphores. Data moves between devices by JAX's collectives and lax.ppermute only.
A program may use at most 128 MiB of HBM per device.

v0:
```python
import functools

import jax
import jax.numpy as jnp
from jax import lax
from jax.experimental import pallas as pl
from jax.experimental.pallas import tpu as pltpu
from jax.sharding import PartitionSpec as P

F32 = jnp.float32
BF16 = jnp.bfloat16
ANY = pl.BlockSpec(memory_space=pl.ANY)
SMEM = pl.BlockSpec(memory_space=pltpu.SMEM)
VMEM = pl.BlockSpec(memory_space=pltpu.VMEM)
SUBLANES = 8
LANES = 128
STEP = 16
MIB = 1 << 20
LITTLE = pl.CostEstimate(flops=1000, bytes_accessed=1000, transcendentals=0)
LONG = pl.CostEstimate(flops=5 * 10**10, bytes_accessed=1000, transcendentals=0)


def in_hbm(array):
    return pltpu.with_memory_space_constraint(array, pltpu.HBM)


def params(mib):
    return pltpu.CompilerParams(vmem_limit_bytes=mib * MIB)


def dot(left, right):
    return jnp.dot(left, right, preferred_element_type=F32)


def dot_nt(left, right):
    return lax.dot_general(left, right, (((1,), (1,)), ((), ())), preferred_element_type=F32)


def choose(index, values):
    out = jnp.int32(values[0])
    for n in range(1, len(values)):
        out = jnp.where(index == n, jnp.int32(values[n]), out)
    return out


def aligned(start, size):
    return pl.ds(pl.multiple_of(start, size), size)


def travel_order(tp_count, rb_count):
    half, quarter = tp_count // 2, tp_count // 4

    def both(distances):
        return [(far, side) for far in distances for side in range(rb_count)]

    long, late = both(range(half, half + quarter)), both(range(half + quarter, tp_count))
    near, rest = both(reversed(range(quarter, half))), both(range(1, quarter))
    own, other = (0, 0), [(0, side) for side in range(1, rb_count)]
    step, part = len(long) // 4, len(rest) // 2
    head = long[: 2 * step] + near[: 2 * step] + long[2 * step : 3 * step]
    tail = rest[:part] + other + near[2 * step : 3 * step] + long[3 * step :] + near[3 * step :] + rest[part:]
    return head, tail, late, [own]


def pick_kernel(keys, times, table, *refs):
    outs, (held, wide, taken_times, sem, times_sem) = refs[:-5], refs[-5:]
    tp_rank, rb_rank = lax.axis_index("tp"), lax.axis_index("rb")
    rows, _, packed, _ = table.shape

    def fetch(chunk):
        where = aligned(chunk * STEP, STEP)
        return pltpu.make_async_copy(table.at[where], held.at[where], sem.at[chunk])

    copy = pltpu.make_async_copy(times, taken_times, times_sem)
    copy.start()
    for chunk in range(rows // STEP):
        fetch(chunk).start()
    copy.wait()

    def step(chunk, carry):
        fetch(chunk).wait()
        where = aligned(chunk * STEP, STEP)
        for n, (far, side) in enumerate(keys):
            time = taken_times[lax.bitwise_xor(rb_rank, side), lax.bitwise_xor(tp_rank, far)]
            slot = n % wide.shape[0]
            wide[slot] = held[where, time].astype(F32).reshape(STEP * packed, LANES)
            for tile in range(packed // 2):
                for part in range(2):
                    taken = wide[slot, pl.ds(2 * tile + part, STEP, stride=packed), :]
                    outs[n][part, where, tile * LANES : (tile + 1) * LANES] = taken.astype(BF16)
        return carry

    lax.fori_loop(0, rows // STEP, step, 0)


def pick(owner_times, peram, keys, name, spare):
    rows, times, parts, width = peram.shape
    tiles = width // LANES
    table = peram.reshape(rows, times, parts, tiles, LANES).swapaxes(2, 3)
    table = table.reshape(rows, times, tiles * parts, LANES)
    picked = pl.pallas_call(
        functools.partial(pick_kernel, keys),
        out_shape=[jax.ShapeDtypeStruct((parts, rows, width), BF16)] * len(keys) + spare,
        in_specs=[ANY, ANY],
        out_specs=[VMEM] * len(keys) + [ANY] * len(spare),
        scratch_shapes=[
            pltpu.VMEM(table.shape, BF16),
            pltpu.VMEM((4, STEP * tiles * parts, LANES), F32),
            pltpu.SMEM(owner_times.shape[::-1], jnp.int32),
            pltpu.SemaphoreType.DMA((rows // STEP,)),
            pltpu.SemaphoreType.DMA,
        ],
        compiler_params=params(32),
        cost_estimate=LITTLE,
        name=name,
    )(in_hbm(owner_times.T), in_hbm(table))
    return dict(zip(keys, picked))


def place(far, per_spin):
    low = lax.axis_index("tp") % per_spin
    return (far // per_spin) * per_spin + lax.bitwise_xor(jnp.int32(far % per_spin), low)


def gram_block(left, right):
    depth = left.shape[1] // 2
    real = dot_nt(left, right)
    imag = dot_nt(left[:, :depth], right[:, depth:]) - dot_nt(left[:, depth:], right[:, :depth])
    return real.astype(BF16), imag.astype(BF16)


def fold(values):
    rows, columns = values.shape
    folded = jnp.sum(values.reshape(rows // SUBLANES, SUBLANES, columns), axis=0)
    return functools.reduce(jnp.add, [folded[:, n : n + LANES] for n in range(0, columns, LANES)])


def direct_sums(diagonal, own, out, carried=None):
    real = functools.reduce(jnp.add, [block[0].astype(F32) for block in diagonal])
    imag = functools.reduce(jnp.add, [block[1].astype(F32) for block in diagonal])
    for slot in range(own.shape[0]):
        elem_re, elem_im = own[slot, 0].astype(F32), own[slot, 1].astype(F32)
        sums = [fold(elem_re * real + elem_im * imag), fold(elem_im * real - elem_re * imag)]
        for part in range(2):
            n = 2 * slot + part
            out[n] = sums[part] if carried is None else sums[part] + carried[n]


def sums_shape(count):
    return jax.ShapeDtypeStruct((count, SUBLANES, LANES), F32)


def early_blocks(spins):
    off = [(s, t) for s in range(spins - 1) for t in range(s + 1, spins - 1)]
    return off + [(s, s) for s in range(spins - 1)]


def early_kernel(eig, keys, rb_count, blocks, *refs):
    pieces, (own, flat, out, traces, sem) = refs[:-5], refs[-5:]
    rows, width = pieces[0].shape[1:]
    depth = rb_count * width
    copies = []
    for n, ((far, side), piece) in enumerate(zip(keys, pieces)):
        where = aligned(place(far, eig // rows) * rows, rows)
        for part in range(2):
            columns = pl.ds(part * depth + side * width, width)
            copies.append(pltpu.make_async_copy(piece.at[part], flat.at[where, columns], sem.at[2 * n + part]))
    for copy in copies:
        copy.start()
    for copy in copies:
        copy.wait()

    def step(n, carry):
        top, side = choose(n, [b[0] for b in blocks]), choose(n, [b[1] for b in blocks])
        out[n, 0], out[n, 1] = gram_block(flat[aligned(top * eig, eig), :], flat[aligned(side * eig, eig), :])
        return carry

    lax.fori_loop(0, len(blocks), step, 0)
    diagonal = [out.at[n] for n, block in enumerate(blocks) if block[0] == block[1]]
    direct_sums(diagonal, own, traces)


def early_gram(keys, pieces, own_elems, spins, eig, rb_count):
    blocks = early_blocks(spins)
    depth = 2 * rb_count * pieces[0].shape[2]
    return pl.pallas_call(
        functools.partial(early_kernel, eig, keys, rb_count, blocks),
        out_shape=(
            jax.ShapeDtypeStruct(((spins - 1) * eig, depth), BF16),
            jax.ShapeDtypeStruct((len(blocks), 2, eig, eig), BF16),
            sums_shape(2 * own_elems.shape[0]),
        ),
        in_specs=[ANY] * len(pieces) + [VMEM],
        out_specs=(VMEM, VMEM, VMEM),
        scratch_shapes=[pltpu.SemaphoreType.DMA((2 * len(pieces),))],
        compiler_params=params(32),
        cost_estimate=LONG,
        name="early_gram",
    )(*pieces, own_elems)


def side_columns(ref, rows, side, width, rb_count):
    return [ref[rows, (part * rb_count + side) * width : (part * rb_count + side + 1) * width] for part in range(2)]


def half_products(left, right):
    real = dot_nt(left[0], right[0]) + dot_nt(left[1], right[1])
    imag = dot_nt(left[0], right[1]) - dot_nt(left[1], right[0])
    return real, imag


def gather_last(eig, keys, others, pieces, last):
    rows, width = pieces[0].shape[1:]
    for (far, _), piece in zip(keys, pieces):
        where = aligned((place(far, eig // rows) - others * (eig // rows)) * rows, rows)
        for part in range(2):
            last[where, part * width : (part + 1) * width] = piece[part]


def late_begin_kernel(eig, keys, rb_count, flat, begun, *refs):
    pieces, (out, last) = refs[:-2], refs[-2:]
    side, width, others = keys[0][1], pieces[0].shape[2], flat.shape[0] // eig
    gather_last(eig, keys, others, pieces, last)
    right = [last[:, :width], last[:, width:]]
    for n in range(others):
        left = side_columns(flat, slice(n * eig, (n + 1) * eig), side, width, rb_count)
        out[n, 0], out[n, 1] = half_products(left, right)
    out[others, 0], out[others, 1] = half_products(right, right)


def late_begin(keys, flat, begun, pieces, spins, eig, rb_count):
    return pl.pallas_call(
        functools.partial(late_begin_kernel, eig, keys, rb_count),
        out_shape=jax.ShapeDtypeStruct((spins, 2, eig, eig), F32),
        in_specs=[VMEM, ANY] + [VMEM] * len(pieces),
        out_specs=VMEM,
        scratch_shapes=[pltpu.VMEM((eig, 2 * pieces[0].shape[2]), BF16)],
        compiler_params=params(32),
        cost_estimate=LITTLE,
        name="late_begin",
    )(flat, begun, *pieces)


def late_rows_kernel(eig, keys, rb_count, flat, partial, *refs):
    pieces, (out, last) = refs[:-2], refs[-2:]
    side, width = keys[0][1], pieces[0].shape[2]
    gather_last(eig, keys, flat.shape[0] // eig, pieces, last)
    right = [last[:, :width], last[:, width:]]
    for n in range(out.shape[0]):
        left = side_columns(flat, slice(n * eig, (n + 1) * eig), side, width, rb_count)
        real, imag = half_products(left, right)
        out[n, 0], out[n, 1] = (partial[n, 0] + real).astype(BF16), (partial[n, 1] + imag).astype(BF16)


def late_rest_kernel(eig, side, rb_count, flat, partial, last, out):
    count, width = out.shape[0] - 1, last.shape[1] // 2
    others = flat.shape[0] // eig
    right = [last[:, :width], last[:, width:]]
    for n in range(count + 1):
        spin = others - count + n
        left = right
        if n < count:
            left = side_columns(flat, slice(spin * eig, (spin + 1) * eig), side, width, rb_count)
        real, imag = half_products(left, right)
        out[n, 0], out[n, 1] = (partial[spin, 0] + real).astype(BF16), (partial[spin, 1] + imag).astype(BF16)


def late_rows(keys, flat, partial, pieces, spins, eig, rb_count):
    return pl.pallas_call(
        functools.partial(late_rows_kernel, eig, keys, rb_count),
        out_shape=(
            jax.ShapeDtypeStruct((spins // 2, 2, eig, eig), BF16),
            jax.ShapeDtypeStruct((eig, 2 * pieces[0].shape[2]), BF16),
        ),
        in_specs=[VMEM] * (2 + len(pieces)),
        out_specs=(VMEM, VMEM),
        compiler_params=params(32),
        cost_estimate=LONG,
        name="late_rows",
    )(flat, partial, *pieces)


def late_rest(side, flat, partial, last, spins, eig, rb_count):
    return pl.pallas_call(
        functools.partial(late_rest_kernel, eig, side, rb_count),
        out_shape=jax.ShapeDtypeStruct((spins - spins // 2, 2, eig, eig), BF16),
        in_specs=[VMEM] * 3,
        out_specs=VMEM,
        compiler_params=params(32),
        cost_estimate=LITTLE,
        name="late_rest",
    )(flat, partial, last)


def factors_kernel(diag_mom, elems, right_ref, left_ref, own_ref, held, sem):
    rank = lax.axis_index("rb")
    eig = held.shape[-1]
    copies = []
    for time in range(2):
        which = diag_mom[0, rank, lax.bitwise_xor(rank, time)]
        copies.append(pltpu.make_async_copy(elems.at[which], held.at[time], sem.at[time]))
    for slot in range(own_ref.shape[0]):
        copies.append(pltpu.make_async_copy(elems.at[diag_mom[0, slot, rank]], own_ref.at[slot], sem.at[2 + slot]))
    for copy in copies:
        copy.start()
    for copy in copies:
        copy.wait()
    for time in range(2):
        re, im = held[time, 0], held[time, 1]
        right_ref[time, :eig, :eig] = re
        right_ref[time, :eig, eig:] = im
        right_ref[time, eig:, :eig] = -im
        right_ref[time, eig:, eig:] = re
        re_t = re.astype(F32).T.astype(BF16)
        im_t = im.astype(F32).T.astype(BF16)
        left_ref[time, :eig, :eig] = re_t
        left_ref[time, :eig, eig:] = im_t
        left_ref[time, eig:, :eig] = im_t
        left_ref[time, eig:, eig:] = -re_t


def factors(diag_mom, src_elems):
    slots, eig = diag_mom.shape[1], src_elems.shape[-1]
    form = jax.ShapeDtypeStruct((2, 2 * eig, 2 * eig), BF16)
    return pl.pallas_call(
        factors_kernel,
        out_shape=(form, form, jax.ShapeDtypeStruct((slots, 2, eig, eig), BF16)),
        in_specs=[SMEM, ANY],
        out_specs=(VMEM, VMEM, VMEM),
        scratch_shapes=[pltpu.VMEM((2, 2, eig, eig), BF16), pltpu.SemaphoreType.DMA((2 + slots,))],
        compiler_params=params(32),
        cost_estimate=LITTLE,
        name="factors",
    )(diag_mom, src_elems)


def late_direct_kernel(rest, own, carried, out):
    direct_sums([rest.at[rest.shape[0] - 1]], own, out, carried)


def late_direct(rest, own, carried):
    return pl.pallas_call(
        late_direct_kernel,
        out_shape=sums_shape(carried.shape[0]),
        in_specs=[VMEM] * 3,
        out_specs=VMEM,
        compiler_params=params(32),
        cost_estimate=LITTLE,
        name="late_direct",
    )(rest, own, carried)


def cross_kernel(offs, own, other, right, left, *refs):
    carried, out = refs[:-1], refs[-1]
    eig = own.shape[-1]
    if len(other.shape) > len(own.shape):
        other = other.at[1 - lax.axis_index("rb")]
    real, imag = [], []

    def add(x, y, count, from_right, from_left):
        rows = [jnp.concatenate([x[n, 0], x[n, 1]], axis=1) for n in range(count)]
        product = dot(jnp.concatenate(rows, axis=0), from_right)
        for n in range(count):
            partner = dot(from_left, y[n].reshape(2 * eig, eig))
            mine = product[n * eig : (n + 1) * eig]
            p_re, p_im = mine[:, :eig], mine[:, eig:]
            w_re, w_im = partner[:eig], partner[eig:]
            real.append(fold(p_re * w_re - p_im * w_im))
            imag.append(fold(p_re * w_im + p_im * w_re))

    add(other, own, own.shape[0], right[1], left[0])
    add(own, other, offs, right[0], left[1])
    out[0] = functools.reduce(jnp.add, real + [ref[0] for ref in carried])
    out[1] = functools.reduce(jnp.add, imag + [ref[1] for ref in carried])


def cross_traces(offs, own, other, right, left, carried, name):
    return pl.pallas_call(
        functools.partial(cross_kernel, offs),
        out_shape=sums_shape(2),
        in_specs=[VMEM] * (4 + len(carried)),
        out_specs=VMEM,
        compiler_params=params(32),
        cost_estimate=LITTLE,
        name=name,
    )(own, other, right, left, *carried)


def last_cross_kernel(offs, own, other, right, left, direct, carried, out):
    count = direct.shape[0]
    for n in range(count):
        out[n] = direct[n]
    cross_kernel(offs, own, other, right, left, carried, out.at[pl.ds(count, 2)])


def last_cross(offs, own, other, right, left, direct, carried):
    return pl.pallas_call(
        functools.partial(last_cross_kernel, offs),
        out_shape=sums_shape(direct.shape[0] + 2),
        in_specs=[VMEM] * 6,
        out_specs=VMEM,
        compiler_params=params(32),
        cost_estimate=LITTLE,
        name="last_cross",
    )(own, other, right, left, direct, carried)


def final_kernel(slots, mine, theirs, count, out):
    rank = lax.axis_index("rb")
    lane = lax.broadcasted_iota(jnp.int32, (1, LANES), 1)

    def totals(ref):
        rows = jnp.concatenate([jnp.sum(ref[n], axis=0, keepdims=True) for n in range(ref.shape[0])], axis=0)
        sums = jnp.broadcast_to(jnp.sum(rows, axis=1, keepdims=True), rows.shape)
        return [sums[n : n + 1] for n in range(ref.shape[0])]

    def put(slot, kind, re, im):
        value = jnp.where(lane == 0, re, im) * 0.25
        out[0, slot, kind : kind + 1, :] = jnp.where(slot < count[0], value, 0.0)[:, :2]

    m, t = totals(mine), totals(theirs)
    for slot in range(slots):
        m_re, m_im, t_re, t_im = m[2 * slot], m[2 * slot + 1], t[2 * slot], t[2 * slot + 1]
        put(slot, 0, m_re * t_re - m_im * t_im, m_re * t_im + m_im * t_re)
        here = rank == slot
        put(slot, 1, jnp.where(here, m[2 * slots], t[2 * slots]), jnp.where(here, m[2 * slots + 1], t[2 * slots + 1]))


def final(mine, theirs, diag_count, slots):
    return pl.pallas_call(
        functools.partial(final_kernel, slots),
        out_shape=jax.ShapeDtypeStruct((1, slots, 2, 2), F32),
        in_specs=[VMEM, VMEM, SMEM],
        out_specs=VMEM,
        compiler_params=params(32),
        name="final",
    )(mine, theirs, diag_count)


def shards(peram, src_elems, owner_times, diag_mom, diag_count):
    tp_count, rb_count = lax.axis_size("tp"), lax.axis_size("rb")
    eig = src_elems.shape[-1]
    spins = tp_count * peram.shape[0] // eig
    slots = diag_mom.shape[1]

    head, tail, late, own = travel_order(tp_count, rb_count)
    early_keys = head + tail
    picked = pick(owner_times, peram, head, "pick_head", [jax.ShapeDtypeStruct((4, *peram.shape), BF16)])
    picked.update(pick(owner_times, peram, tail + late + own, "pick_tail", []))

    def send(key):
        far, side = key
        pairs = [
            (tp * rb_count + rb, (tp ^ far) * rb_count + (rb ^ side))
            for tp in range(tp_count)
            for rb in range(rb_count)
        ]
        return lax.ppermute(picked[key], ("tp", "rb"), pairs)

    swap = [(rb, rb ^ 1) for rb in range(rb_count)]
    right, left, own_elems = factors(diag_mom, src_elems)
    arrived = [send(key) for key in early_keys] + [picked[key] for key in own]
    flat, early, direct = early_gram(early_keys + own, arrived, own_elems, spins, eig, rb_count)
    early_both = lax.all_to_all(jnp.stack([early] * rb_count), "rb", 0, 0)
    offs = early.shape[0] - (spins - 1)
    begun = cross_traces(offs, early, early_both, right, left, [], "early_cross")

    halves = [[key for key in late if key[1] == side] for side in range(rb_count)]
    sent = [[send(key) for key in keys] for keys in halves]
    half = late_begin(halves[0], flat, begun, sent[0], spins, eig, rb_count)
    blocks, last = late_rows(halves[1], flat, half, sent[1], spins, eig, rb_count)
    swapped = lax.ppermute(blocks, "rb", swap)
    rest = late_rest(1, flat, half, last, spins, eig, rb_count)
    rest_swapped = lax.ppermute(rest, "rb", swap)
    traces = late_direct(rest, own_elems, direct)
    partial = cross_traces(blocks.shape[0], blocks, swapped, right, left, [begun], "late_cross")
    mine = last_cross(rest.shape[0] - 1, rest, rest_swapped, right, left, traces, partial)
    theirs = lax.ppermute(mine, "rb", swap)
    return final(mine, theirs, diag_count, slots)


def solution(mesh):
    in_specs = (
        P(("grp", "tp"), None, None, "rb"),
        P("grp", None, None, None),
        P("grp", None),
        P(("grp", "tp"), None, None),
        P(("grp", "tp")),
    )
    out_specs = P(("grp", "tp"), None, None, None)
    return jax.shard_map(shards, mesh=mesh, in_specs=in_specs, out_specs=out_specs, check_vma=False)
```

profile of v0, /device:TPU:11, one launch (start us, length us, event | category | flops | bytes accessed | tf_op | source)
XLA Modules:
  0.0 103.4 jit_solution(17809311534606986408)
XLA Ops:
  0.0 3.0 %pick_head.1 = (bf16[2,128,512]{2,1,0:T(8,128)(2,1)S(1)}, bf16[2,128,512]{2,1,0:T(8,128)(2,1)S(1)}, bf16[2,128,512]{2,1,0:T(8,128)(2,1)S(1)}, bf16[2,128,512]{2,...) custom-call(s32[2,8]{1,0:T(2,128)} %bitcast.10, ...), custom_call_target="tpu_custom_call" | custom-call | flops 1000 | bytes 1000 | tf_op jit(solution)/shard_map/pick_head/pallas_call | solution.py:101
  3.0 2.4 %collective-permute-start = (bf16[2,128,512]{2,1,0:T(8,128)(2,1)S(1)}, bf16[2,128,512]{2,1,0:T(8,128)(2,1)S(1)}, u32[]{:S(2)}, u32[]{:S(2)}) collective-permute-start(bf16[2,128,512]{2,1,0:T(8,128)(2,1)S(1)} %get-tuple-element.29), channel_id=1, source_target_pairs={{0,8},{1,9},{2,10},{3,11},{4,12},{5,13},{6,14},{7,15},{8,0},{9,1},... | collective-permute-start | bytes 786440 | tf_op jit(solution)/shard_map/ppermute | solution.py:458
  5.4 0.9 collective-permute-start.1
  6.3 1.1 %collective-permute-start.2 = (bf16[2,128,512]{2,1,0:T(8,128)(2,1)S(1)}, bf16[2,128,512]{2,1,0:T(8,128)(2,1)S(1)}, u32[]{:S(2)}, u32[]{:S(2)}) collective-permute-start(bf16[2,128,512]{2,1,0:T(8,128)(2,1)S(1)} %get-tuple-element.31), channel_id=1, source_target_pairs={{0,6},{1,7},{2,4},{3,5},{4,2},{5,3},{6,0},{7,1},{8,14},{9,15},{10,... | collective-permute-start | bytes 786440 | tf_op jit(solution)/shard_map/ppermute | solution.py:458
  7.4 1.5 %collective-permute-start.3 = (bf16[2,128,512]{2,1,0:T(8,128)(2,1)S(1)}, bf16[2,128,512]{2,1,0:T(8,128)(2,1)S(1)}, u32[]{:S(2)}, u32[]{:S(2)}) collective-permute-start(bf16[2,128,512]{2,1,0:T(8,128)(2,1)S(1)} %get-tuple-element.32), channel_id=1, source_target_pairs={{0,7},{1,6},{2,5},{3,4},{4,3},{5,2},{6,1},{7,0},{8,15},{9,14},{10,... | collective-permute-start | bytes 786440 | tf_op jit(solution)/shard_map/ppermute | solution.py:458
  8.9 2.8 %collective-permute-start.4 = (bf16[2,128,512]{2,1,0:T(8,128)(2,1)S(1)}, bf16[2,128,512]{2,1,0:T(8,128)(2,1)S(1)}, u32[]{:S(2)}, u32[]{:S(2)}) collective-permute-start(bf16[2,128,512]{2,1,0:T(8,128)(2,1)S(1)} %get-tuple-element.33), channel_id=1, source_target_pairs={{0,10},{1,11},{2,8},{3,9},{4,14},{5,15},{6,12},{7,13},{8,2},{9,3},... | collective-permute-start | bytes 786440 | tf_op jit(solution)/shard_map/ppermute | solution.py:458
  11.6 3.2 %pick_tail.1 = (bf16[2,128,512]{2,1,0:T(8,128)(2,1)S(1)}, bf16[2,128,512]{2,1,0:T(8,128)(2,1)S(1)}, bf16[2,128,512]{2,1,0:T(8,128)(2,1)S(1)}, bf16[2,128,512]{2,...) custom-call(s32[2,8]{1,0:T(2,128)} %bitcast.11, ...), custom_call_target="tpu_custom_call" | custom-call | flops 1000 | bytes 1000 | tf_op jit(solution)/shard_map/pick_tail/pallas_call | solution.py:101
  14.8 7.7 %collective-permute-done.refs_0_ = bf16[2,128,512]{2,1,0:T(8,128)(2,1)S(1)} collective-permute-done((bf16[2,128,512]{2,1,0:T(8,128)(2,1)S(1)}, bf16[2,128,512]{2,1,0:T(8,128)(2,1)S(1)}, u32[]{:S(2)}, u32[]{:S(2)}) %collective-permute-start) | collective-permute-done | bytes 262176 | tf_op jit(solution)/shard_map/ppermute | solution.py:458
  22.6 1.2 %collective-permute-start.5 = (bf16[2,128,512]{2,1,0:T(8,128)(2,1)S(1)}, bf16[2,128,512]{2,1,0:T(8,128)(2,1)S(1)}, u32[]{:S(2)}, u32[]{:S(2)}) collective-permute-start(bf16[2,128,512]{2,1,0:T(8,128)(2,1)S(1)} %get-tuple-element.34), channel_id=1, source_target_pairs={{0,2},{1,3},{2,0},{3,1},{4,6},{5,7},{6,4},{7,5},{8,10},{9,11},{10,... | collective-permute-start | bytes 786440 | tf_op jit(solution)/shard_map/ppermute | solution.py:458
  23.8 4.9 %collective-permute-done.1.refs_1_ = bf16[2,128,512]{2,1,0:T(8,128)(2,1)S(1)} collective-permute-done((bf16[2,128,512]{2,1,0:T(8,128)(2,1)S(1)}, bf16[2,128,512]{2,1,0:T(8,128)(2,1)S(1)}, u32[]{:S(2)}, u32[]{:S(2)}) %collective-permute-start.1) | collective-permute-done | bytes 262176 | tf_op jit(solution)/shard_map/ppermute | solution.py:458
  28.7 0.9 collective-permute-start.6
  29.6 1.9 %collective-permute-start.7 = (bf16[2,128,512]{2,1,0:T(8,128)(2,1)S(1)}, bf16[2,128,512]{2,1,0:T(8,128)(2,1)S(1)}, u32[]{:S(2)}, u32[]{:S(2)}) collective-permute-start(bf16[2,128,512]{2,1,0:T(8,128)(2,1)S(1)} %get-tuple-element.36), channel_id=1, source_target_pairs={{0,4},{1,5},{2,6},{3,7},{4,0},{5,1},{6,2},{7,3},{8,12},{9,13},{10,... | collective-permute-start | bytes 786440 | tf_op jit(solution)/shard_map/ppermute | solution.py:458
  31.5 4.4 %collective-permute-start.8 = (bf16[2,128,512]{2,1,0:T(8,128)(2,1)S(1)}, bf16[2,128,512]{2,1,0:T(8,128)(2,1)S(1)}, u32[]{:S(2)}, u32[]{:S(2)}) collective-permute-start(bf16[2,128,512]{2,1,0:T(8,128)(2,1)S(1)} %get-tuple-element.37), channel_id=1, source_target_pairs={{0,11},{1,10},{2,9},{3,8},{4,15},{5,14},{6,13},{7,12},{8,3},{9,2},... | collective-permute-start | bytes 786440 | tf_op jit(solution)/shard_map/ppermute | solution.py:458
  36.0 4.0 %collective-permute-done.4.refs_4_ = bf16[2,128,512]{2,1,0:T(8,128)(2,1)S(1)} collective-permute-done((bf16[2,128,512]{2,1,0:T(8,128)(2,1)S(1)}, bf16[2,128,512]{2,1,0:T(8,128)(2,1)S(1)}, u32[]{:S(2)}, u32[]{:S(2)}) %collective-permute-start.4) | collective-permute-done | bytes 262176 | tf_op jit(solution)/shard_map/ppermute | solution.py:458
  40.0 3.9 %collective-permute-start.9 = (bf16[2,128,512]{2,1,0:T(8,128)(2,1)S(1)}, bf16[2,128,512]{2,1,0:T(8,128)(2,1)S(1)}, u32[]{:S(2)}, u32[]{:S(2)}) collective-permute-start(bf16[2,128,512]{2,1,0:T(8,128)(2,1)S(1)} %get-tuple-element.38), channel_id=1, source_target_pairs={{0,5},{1,4},{2,7},{3,6},{4,1},{5,0},{6,3},{7,2},{8,13},{9,12},{10,... | collective-permute-start | bytes 786440 | tf_op jit(solution)/shard_map/ppermute | solution.py:458
  43.9 0.9 factors.1
  44.8 1.6 %collective-permute-start.11 = (bf16[2,128,512]{2,1,0:T(8,128)(2,1)S(1)}, bf16[2,128,512]{2,1,0:T(8,128)(2,1)S(1)}, u32[]{:S(2)}, u32[]{:S(2)}) collective-permute-start(bf16[2,128,512]{2,1,0:T(8,128)(2,1)S(1)} %get-tuple-element.46), channel_id=1, source_target_pairs={{0,12},{1,13},{2,14},{3,15},{4,8},{5,9},{6,10},{7,11},{8,4},{9,5},... | collective-permute-start | bytes 786440 | tf_op jit(solution)/shard_map/ppermute | solution.py:458
  46.4 0.9 collective-permute-start.12
  47.4 3.9 %collective-permute-done.8.refs_8_ = bf16[2,128,512]{2,1,0:T(8,128)(2,1)S(1)} collective-permute-done((bf16[2,128,512]{2,1,0:T(8,128)(2,1)S(1)}, bf16[2,128,512]{2,1,0:T(8,128)(2,1)S(1)}, u32[]{:S(2)}, u32[]{:S(2)}) %collective-permute-start.8) | collective-permute-done | bytes 262176 | tf_op jit(solution)/shard_map/ppermute | solution.py:458
  51.5 18.7 %collective-permute-done.9.refs_9_ = bf16[2,128,512]{2,1,0:T(8,128)(2,1)S(1)} collective-permute-done((bf16[2,128,512]{2,1,0:T(8,128)(2,1)S(1)}, bf16[2,128,512]{2,1,0:T(8,128)(2,1)S(1)}, u32[]{:S(2)}, u32[]{:S(2)}) %collective-permute-start.9) | collective-permute-done | bytes 262176 | tf_op jit(solution)/shard_map/ppermute | solution.py:458
  70.2 3.8 %collective-permute-start.14 = (bf16[2,128,512]{2,1,0:T(8,128)(2,1)S(1)}, bf16[2,128,512]{2,1,0:T(8,128)(2,1)S(1)}, u32[]{:S(2)}, u32[]{:S(2)}) collective-permute-start(bf16[2,128,512]{2,1,0:T(8,128)(2,1)S(1)} %get-tuple-element.49), channel_id=1, source_target_pairs={{0,15},{1,14},{2,13},{3,12},{4,11},{5,10},{6,9},{7,8},{8,7},{9,6},... | collective-permute-start | bytes 786440 | tf_op jit(solution)/shard_map/ppermute | solution.py:458
  74.0 5.6 %early_gram.1 = (bf16[768,2048]{1,0:T(8,128)(2,1)S(1)}, bf16[6,2,256,256]{3,2,1,0:T(8,128)(2,1)S(1)}, f32[4,8,128]{2,1,0:T(8,128)S(1)}) custom-call(bf16[2,128,512]{2,1,0:T(8,128)(2,1)S(1)} %collective-permute-done.refs_0_, bf16[2,128,512]{2,1,0:T(8,128)(2,1)S(1)} %collective-permute-done.1.refs_1_, bf16[2,128,512]{2,1,0:T(8,128)(2,1)S(1)} %collective-permute-done.2.refs_2_, ...), custom_call_target="tpu_custom_call" | custom-call | flops 49999998976 | bytes 1000 | tf_op jit(solution)/shard_map/early_gram/pallas_call | solution.py:186
  79.9 6.1 %all_to_all.5.other = bf16[2,6,2,256,256]{4,3,2,1,0:T(8,128)(2,1)S(1)} all-to-all(bf16[2,6,2,256,256]{4,3,2,1,0:T(8,128)(2,1)S(1)} %pad_maximum_fusion), channel_id=1, replica_groups=mesh['grp'=2,'tp'=8,'rb'=2] {'rb'}, dimensions={0} | all-to-all | bytes 6291456 | tf_op jit(solution)/shard_map/all_to_all | solution.py:464
  86.0 2.7 %early_cross.1.begun.refs_0_ = f32[2,8,128]{2,1,0:T(8,128)S(1)} custom-call(bf16[6,2,256,256]{3,2,1,0:T(8,128)(2,1)S(1)} %get-tuple-element.43.own, bf16[2,6,2,256,256]{4,3,2,1,0:T(8,128)(2,1)S(1)} %all_to_all.5.other, bf16[2,512,512]{2,1,0:T(8,128)(2,1)S(1)} %get-tuple-element.44.right, bf16[2,512,512]{2,1,0:T(8,128)(2,1)S(1)} %get-tuple-element.45.left), custom_call_target="tpu_custom_call" | custom-call | flops 1000 | bytes 1000 | tf_op jit(solution)/shard_map/early_cross/pallas_call | solution.py:378
  88.7 1.4 %late_begin.1.partial = f32[4,2,256,256]{3,2,1,0:T(8,128)S(1)} custom-call(bf16[768,2048]{1,0:T(8,128)(2,1)S(1)} %get-tuple-element.42.flat, f32[2,8,128]{2,1,0:T(8,128)S(1)} %early_cross.1.begun.refs_0_, bf16[2,128,512]{2,1,0:T(8,128)(2,1)S(1)} %collective-permute-done.11.refs_0_, bf16[2,128,512]{2,1,0:T(8,128)(2,1)S(1)} %collective-permute-done.12.refs_1_), custom_call_target="tpu_custom_call" | custom-call | flops 1000 | bytes 1000 | tf_op jit(solution)/shard_map/late_begin/pallas_call | solution.py:232
  90.1 1.1 %collective-permute-done.13.refs_0_ = bf16[2,128,512]{2,1,0:T(8,128)(2,1)S(1)} collective-permute-done((bf16[2,128,512]{2,1,0:T(8,128)(2,1)S(1)}, bf16[2,128,512]{2,1,0:T(8,128)(2,1)S(1)}, u32[]{:S(2)}, u32[]{:S(2)}) %collective-permute-start.13) | collective-permute-done | bytes 262176 | tf_op jit(solution)/shard_map/ppermute | solution.py:458
  91.2 5.1 %collective-permute-done.14.refs_1_ = bf16[2,128,512]{2,1,0:T(8,128)(2,1)S(1)} collective-permute-done((bf16[2,128,512]{2,1,0:T(8,128)(2,1)S(1)}, bf16[2,128,512]{2,1,0:T(8,128)(2,1)S(1)}, u32[]{:S(2)}, u32[]{:S(2)}) %collective-permute-start.14) | collective-permute-done | bytes 262176 | tf_op jit(solution)/shard_map/ppermute | solution.py:458
  96.3 0.8 late_rows.1
  97.2 0.8 late_rest.1.rest.own
  99.1 1.3 %late_cross.1.carried = f32[2,8,128]{2,1,0:T(8,128)S(1)} custom-call(bf16[2,2,256,256]{3,2,1,0:T(8,128)(2,1)S(1)} %get-tuple-element.52.own, bf16[2,2,256,256]{3,2,1,0:T(8,128)(2,1)S(1)} %collective-permute-done.16.other, bf16[2,512,512]{2,1,0:T(8,128)(2,1)S(1)} %get-tuple-element.44.right, bf16[2,512,512]{2,1,0:T(8,128)(2,1)S(1)} %get-tuple-element.45.left, ...), custom_call_target="tpu_custom_call" | custom-call | flops 1000 | bytes 1000 | tf_op jit(solution)/shard_map/late_cross/pallas_call | solution.py:378
  100.4 1.0 last_cross.1.mine
  102.7 0.7 final.1
  (22 shorter events, 2.3 us)
Async XLA Ops:
  3.0 19.6 %collective-permute-start = (bf16[2,128,512]{2,1,0:T(8,128)(2,1)S(1)}, bf16[2,128,512]{2,1,0:T(8,128)(2,1)S(1)}, u32[]{:S(2)}, u32[]{:S(2)}) collective-permute-start(bf16[2,128,512]{2,1,0:T(8,128)(2,1)S(1)} %get-tuple-element.29), channel_id=1, source_target_pairs={{0,8},{1,9},{2,10},{3,11},{4,12},{5,13},{6,14},{7,15},{8,0},{9,1},... | collective-permute-start | bytes 786440 | tf_op jit(solution)/shard_map/ppermute | solution.py:458
  5.4 23.3 %collective-permute-start.1 = (bf16[2,128,512]{2,1,0:T(8,128)(2,1)S(1)}, bf16[2,128,512]{2,1,0:T(8,128)(2,1)S(1)}, u32[]{:S(2)}, u32[]{:S(2)}) collective-permute-start(bf16[2,128,512]{2,1,0:T(8,128)(2,1)S(1)} %get-tuple-element.30), channel_id=1, source_target_pairs={{0,9},{1,8},{2,11},{3,10},{4,13},{5,12},{6,15},{7,14},{8,1},{9,0},... | collective-permute-start | bytes 786440 | tf_op jit(solution)/shard_map/ppermute | solution.py:458
  6.3 23.4 %collective-permute-start.2 = (bf16[2,128,512]{2,1,0:T(8,128)(2,1)S(1)}, bf16[2,128,512]{2,1,0:T(8,128)(2,1)S(1)}, u32[]{:S(2)}, u32[]{:S(2)}) collective-permute-start(bf16[2,128,512]{2,1,0:T(8,128)(2,1)S(1)} %get-tuple-element.31), channel_id=1, source_target_pairs={{0,6},{1,7},{2,4},{3,5},{4,2},{5,3},{6,0},{7,1},{8,14},{9,15},{10,... | collective-permute-start | bytes 786440 | tf_op jit(solution)/shard_map/ppermute | solution.py:458
  7.4 24.1 %collective-permute-start.3 = (bf16[2,128,512]{2,1,0:T(8,128)(2,1)S(1)}, bf16[2,128,512]{2,1,0:T(8,128)(2,1)S(1)}, u32[]{:S(2)}, u32[]{:S(2)}) collective-permute-start(bf16[2,128,512]{2,1,0:T(8,128)(2,1)S(1)} %get-tuple-element.32), channel_id=1, source_target_pairs={{0,7},{1,6},{2,5},{3,4},{4,3},{5,2},{6,1},{7,0},{8,15},{9,14},{10,... | collective-permute-start | bytes 786440 | tf_op jit(solution)/shard_map/ppermute | solution.py:458
  8.9 35.1 %copy-start = (bf16[7,2,256,256]{3,2,1,0:T(8,128)(2,1)S(1)}, bf16[7,2,256,256]{3,2,1,0:T(8,128)(2,1)}, u32[]{:S(2)}) copy-start(bf16[7,2,256,256]{3,2,1,0:T(8,128)(2,1)} %elems.1) | copy-start | bytes 5505028
  8.9 35.1 %copy-start.1 = (s32[1,2,2]{2,1,0:T(2,128)S(1)}, s32[1,2,2]{2,1,0:T(2,128)}, u32[]{:S(2)}) copy-start(s32[1,2,2]{2,1,0:T(2,128)} %diag_mom.1) | copy-start | bytes 52
  8.9 31.1 %collective-permute-start.4 = (bf16[2,128,512]{2,1,0:T(8,128)(2,1)S(1)}, bf16[2,128,512]{2,1,0:T(8,128)(2,1)S(1)}, u32[]{:S(2)}, u32[]{:S(2)}) collective-permute-start(bf16[2,128,512]{2,1,0:T(8,128)(2,1)S(1)} %get-tuple-element.33), channel_id=1, source_target_pairs={{0,10},{1,11},{2,8},{3,9},{4,14},{5,15},{6,12},{7,13},{8,2},{9,3},... | collective-permute-start | bytes 786440 | tf_op jit(solution)/shard_map/ppermute | solution.py:458
  22.6 21.3 %collective-permute-start.5 = (bf16[2,128,512]{2,1,0:T(8,128)(2,1)S(1)}, bf16[2,128,512]{2,1,0:T(8,128)(2,1)S(1)}, u32[]{:S(2)}, u32[]{:S(2)}) collective-permute-start(bf16[2,128,512]{2,1,0:T(8,128)(2,1)S(1)} %get-tuple-element.34), channel_id=1, source_target_pairs={{0,2},{1,3},{2,0},{3,1},{4,6},{5,7},{6,4},{7,5},{8,10},{9,11},{10,... | collective-permute-start | bytes 786440 | tf_op jit(solution)/shard_map/ppermute | solution.py:458
  28.7 16.2 %collective-permute-start.6 = (bf16[2,128,512]{2,1,0:T(8,128)(2,1)S(1)}, bf16[2,128,512]{2,1,0:T(8,128)(2,1)S(1)}, u32[]{:S(2)}, u32[]{:S(2)}) collective-permute-start(bf16[2,128,512]{2,1,0:T(8,128)(2,1)S(1)} %get-tuple-element.35), channel_id=1, source_target_pairs={{0,1},{1,0},{2,3},{3,2},{4,5},{5,4},{6,7},{7,6},{8,9},{9,8},{10,11... | collective-permute-start | bytes 786440 | tf_op jit(solution)/shard_map/ppermute | solution.py:458
  29.6 16.8 %collective-permute-start.7 = (bf16[2,128,512]{2,1,0:T(8,128)(2,1)S(1)}, bf16[2,128,512]{2,1,0:T(8,128)(2,1)S(1)}, u32[]{:S(2)}, u32[]{:S(2)}) collective-permute-start(bf16[2,128,512]{2,1,0:T(8,128)(2,1)S(1)} %get-tuple-element.36), channel_id=1, source_target_pairs={{0,4},{1,5},{2,6},{3,7},{4,0},{5,1},{6,2},{7,3},{8,12},{9,13},{10,... | collective-permute-start | bytes 786440 | tf_op jit(solution)/shard_map/ppermute | solution.py:458
  31.5 19.7 %collective-permute-start.8 = (bf16[2,128,512]{2,1,0:T(8,128)(2,1)S(1)}, bf16[2,128,512]{2,1,0:T(8,128)(2,1)S(1)}, u32[]{:S(2)}, u32[]{:S(2)}) collective-permute-start(bf16[2,128,512]{2,1,0:T(8,128)(2,1)S(1)} %get-tuple-element.37), channel_id=1, source_target_pairs={{0,11},{1,10},{2,9},{3,8},{4,15},{5,14},{6,13},{7,12},{8,3},{9,2},... | collective-permute-start | bytes 786440 | tf_op jit(solution)/shard_map/ppermute | solution.py:458
  40.0 30.2 %collective-permute-start.9 = (bf16[2,128,512]{2,1,0:T(8,128)(2,1)S(1)}, bf16[2,128,512]{2,1,0:T(8,128)(2,1)S(1)}, u32[]{:S(2)}, u32[]{:S(2)}) collective-permute-start(bf16[2,128,512]{2,1,0:T(8,128)(2,1)S(1)} %get-tuple-element.38), channel_id=1, source_target_pairs={{0,5},{1,4},{2,7},{3,6},{4,1},{5,0},{6,3},{7,2},{8,13},{9,12},{10,... | collective-permute-start | bytes 786440 | tf_op jit(solution)/shard_map/ppermute | solution.py:458
  43.9 30.1 %collective-permute-start.10 = (bf16[2,128,512]{2,1,0:T(8,128)(2,1)S(1)}, bf16[2,128,512]{2,1,0:T(8,128)(2,1)S(1)}, u32[]{:S(2)}, u32[]{:S(2)}) collective-permute-start(bf16[2,128,512]{2,1,0:T(8,128)(2,1)S(1)} %get-tuple-element.39), channel_id=1, source_target_pairs={{0,3},{1,2},{2,1},{3,0},{4,7},{5,6},{6,5},{7,4},{8,11},{9,10},{10,... | collective-permute-start | bytes 786440 | tf_op jit(solution)/shard_map/ppermute | solution.py:458
  44.8 43.8 %collective-permute-start.11 = (bf16[2,128,512]{2,1,0:T(8,128)(2,1)S(1)}, bf16[2,128,512]{2,1,0:T(8,128)(2,1)S(1)}, u32[]{:S(2)}, u32[]{:S(2)}) collective-permute-start(bf16[2,128,512]{2,1,0:T(8,128)(2,1)S(1)} %get-tuple-element.46), channel_id=1, source_target_pairs={{0,12},{1,13},{2,14},{3,15},{4,8},{5,9},{6,10},{7,11},{8,4},{9,5},... | collective-permute-start | bytes 786440 | tf_op jit(solution)/shard_map/ppermute | solution.py:458
  46.4 42.2 %collective-permute-start.12 = (bf16[2,128,512]{2,1,0:T(8,128)(2,1)S(1)}, bf16[2,128,512]{2,1,0:T(8,128)(2,1)S(1)}, u32[]{:S(2)}, u32[]{:S(2)}) collective-permute-start(bf16[2,128,512]{2,1,0:T(8,128)(2,1)S(1)} %get-tuple-element.47), channel_id=1, source_target_pairs={{0,14},{1,15},{2,12},{3,13},{4,10},{5,11},{6,8},{7,9},{8,6},{9,7},... | collective-permute-start | bytes 786440 | tf_op jit(solution)/shard_map/ppermute | solution.py:458
  51.2 39.9 %collective-permute-start.13 = (bf16[2,128,512]{2,1,0:T(8,128)(2,1)S(1)}, bf16[2,128,512]{2,1,0:T(8,128)(2,1)S(1)}, u32[]{:S(2)}, u32[]{:S(2)}) collective-permute-start(bf16[2,128,512]{2,1,0:T(8,128)(2,1)S(1)} %get-tuple-element.48), channel_id=1, source_target_pairs={{0,13},{1,12},{2,15},{3,14},{4,9},{5,8},{6,11},{7,10},{8,5},{9,4},... | collective-permute-start | bytes 786440 | tf_op jit(solution)/shard_map/ppermute | solution.py:458
  70.2 26.1 %collective-permute-start.14 = (bf16[2,128,512]{2,1,0:T(8,128)(2,1)S(1)}, bf16[2,128,512]{2,1,0:T(8,128)(2,1)S(1)}, u32[]{:S(2)}, u32[]{:S(2)}) collective-permute-start(bf16[2,128,512]{2,1,0:T(8,128)(2,1)S(1)} %get-tuple-element.49), channel_id=1, source_target_pairs={{0,15},{1,14},{2,13},{3,12},{4,11},{5,10},{6,9},{7,8},{8,7},{9,6},... | collective-permute-start | bytes 786440 | tf_op jit(solution)/shard_map/ppermute | solution.py:458
  97.1 2.0 %collective-permute-start.16 = (bf16[2,2,256,256]{3,2,1,0:T(8,128)(2,1)S(1)}, bf16[2,2,256,256]{3,2,1,0:T(8,128)(2,1)S(1)}, u32[]{:S(2)}, u32[]{:S(2)}) collective-permute-start(bf16[2,2,256,256]{3,2,1,0:T(8,128)(2,1)S(1)} %get-tuple-element.52.own), channel_id=1, source_target_pairs={{0,1},{1,0},{2,3},{3,2},{4,5},{5,4},{6,7},{7,6},{8,9},{9,8},{10,11... | collective-permute-start | bytes 1572872 | tf_op jit(solution)/shard_map/ppermute | solution.py:472
  98.0 2.4 %collective-permute-start.15 = (bf16[2,2,256,256]{3,2,1,0:T(8,128)(2,1)S(1)}, bf16[2,2,256,256]{3,2,1,0:T(8,128)(2,1)S(1)}, u32[]{:S(2)}, u32[]{:S(2)}) collective-permute-start(bf16[2,2,256,256]{3,2,1,0:T(8,128)(2,1)S(1)} %late_rest.1.rest.own), channel_id=1, source_target_pairs={{0,1},{1,0},{2,3},{3,2},{4,5},{5,4},{6,7},{7,6},{8,9},{9,8},{10,11... | collective-permute-start | bytes 1572872 | tf_op jit(solution)/shard_map/ppermute | solution.py:474
  101.4 1.3 %collective-permute-start.17 = (f32[6,8,128]{2,1,0:T(8,128)S(1)}, f32[6,8,128]{2,1,0:T(8,128)S(1)}, u32[]{:S(2)}, u32[]{:S(2)}) collective-permute-start(f32[6,8,128]{2,1,0:T(8,128)S(1)} %last_cross.1.mine), channel_id=1, source_target_pairs={{0,1},{1,0},{2,3},{3,2},{4,5},{5,4},{6,7},{7,6},{8,9},{9,8},{10,11... | collective-permute-start | bytes 73736 | tf_op jit(solution)/shard_map/ppermute | solution.py:478
where the time goes:
time: 105 us; the launch traced here: 103 us
  waiting for transfers between devices  46.1 us (44%)
  starting transfers between devices  28.4 us (27%)
  Pallas kernels  21.7 us (21%)
  blocking collectives  6.1 us (6%)
    ppermute x15, waiting for transfers between devices, send(): return lax.ppermute(picked[key], ('tp', 'rb'), pairs)  45.5 us
    ppermute x15, starting transfers between devices, send(): return lax.ppermute(picked[key], ('tp', 'rb'), pairs)  27.6 us
    pallas_call x2, Pallas kernels, pick(): pl.pallas_call(functools.partial(pick_kernel, keys), out_shape=[jax.Shape...  6.19 us
    all_to_all x1, blocking collectives, shards(): early_both = lax.all_to_all(jnp.stack([early] * rb_count), 'rb', 0, 0)  6.1 us
    pallas_call x1, Pallas kernels, early_gram(): pl.pallas_call(functools.partial(early_kernel, eig, keys, rb_count, block...  5.57 us
    pallas_call x2, Pallas kernels, cross_traces(): pl.pallas_call(functools.partial(cross_kernel, offs), out_shape=sums_shap...  4.02 us
  transfers between devices with their start and end apart: 18, of which 9 were waited for; matrix products, arithmetic and copies ran while one was open for 0% of the time, Pallas kernels for 16%

commit v1 on v0

--- a/solution.py
+++ b/solution.py
@@ -62,6 +62,12 @@
     return head, tail, late, [own]
 
 
+def distance(far, tp_rank, tp_count):
+    if far < tp_count // 2:
+        return far
+    return lax.bitwise_xor(jnp.int32(far), jnp.where(tp_rank < tp_count // 2, jnp.int32(tp_count // 4), jnp.int32(0)))
+
+
 def pick_kernel(keys, times, table, *refs):
     outs, (held, wide, taken_times, sem, times_sem) = refs[:-5], refs[-5:]
     tp_rank, rb_rank = lax.axis_index("tp"), lax.axis_index("rb")
@@ -81,7 +87,8 @@
         fetch(chunk).wait()
         where = aligned(chunk * STEP, STEP)
         for n, (far, side) in enumerate(keys):
-            time = taken_times[lax.bitwise_xor(rb_rank, side), lax.bitwise_xor(tp_rank, far)]
+            owner = lax.bitwise_xor(tp_rank, distance(far, tp_rank, taken_times.shape[1]))
+            time = taken_times[lax.bitwise_xor(rb_rank, side), owner]
             slot = n % wide.shape[0]
             wide[slot] = held[where, time].astype(F32).reshape(STEP * packed, LANES)
             for tile in range(packed // 2):
@@ -450,8 +457,9 @@
 
     def send(key):
         far, side = key
+        swapped = tp_count // 4 if far >= tp_count // 2 else 0
         pairs = [
-            (tp * rb_count + rb, (tp ^ far) * rb_count + (rb ^ side))
+            (tp * rb_count + rb, (tp ^ far ^ (swapped if tp < tp_count // 2 else 0)) * rb_count + (rb ^ side))
             for tp in range(tp_count)
             for rb in range(rb_count)
         ]

time: 105 us -> 104 us (level)
  starting transfers between devices: 28.4 us -> 25.8 us
  waiting for transfers between devices: 46.1 us -> 48.3 us
    ppermute x15, starting transfers between devices: 27.6 us -> 25 us  [send(): return lax.ppermute(picked[key], ('tp', 'rb'), pairs)]
    ppermute x15, waiting for transfers between devices: 45.5 us -> 47.7 us  [send(): return lax.ppermute(picked[key], ('tp', 'rb'), pairs)]
  transfers between devices with their start and end apart: 18 -> 18, of which waited for: 9 -> 11; matrix products, arithmetic and copies ran while one was open for 0% -> 0% of each run, Pallas kernels for 16% -> 16%
where the time goes in v1:
time: 104 us; the launch traced here: 103 us
  waiting for transfers between devices  48.3 us (46%)
  starting transfers between devices  25.8 us (25%)
  Pallas kernels  21.7 us (21%)
  blocking collectives  6.49 us (6%)
    ppermute x15, waiting for transfers between devices, send(): return lax.ppermute(picked[key], ('tp', 'rb'), pairs)  47.7 us
    ppermute x15, starting transfers between devices, send(): return lax.ppermute(picked[key], ('tp', 'rb'), pairs)  25 us
    all_to_all x1, blocking collectives, shards(): early_both = lax.all_to_all(jnp.stack([early] * rb_count), 'rb', 0, 0)  6.49 us
    pallas_call x2, Pallas kernels, pick(): pl.pallas_call(functools.partial(pick_kernel, keys), out_shape=[jax.Shape...  6.19 us
    pallas_call x1, Pallas kernels, early_gram(): pl.pallas_call(functools.partial(early_kernel, eig, keys, rb_count, block...  5.57 us
    pallas_call x2, Pallas kernels, cross_traces(): pl.pallas_call(functools.partial(cross_kernel, offs), out_shape=sums_shap...  4.02 us
  transfers between devices with their start and end apart: 18, of which 11 were waited for; matrix products, arithmetic and copies ran while one was open for 0% of the time, Pallas kernels for 16%

profile of v1, /device:TPU:11, one launch (start us, length us, event | category | flops | bytes accessed | tf_op | source)
XLA Modules:
  0.0 103.4 jit_solution(14552904950628484619)
XLA Ops:
  0.0 3.0 %pick_head.1 = (bf16[2,128,512]{2,1,0:T(8,128)(2,1)S(1)}, bf16[2,128,512]{2,1,0:T(8,128)(2,1)S(1)}, bf16[2,128,512]{2,1,0:T(8,128)(2,1)S(1)}, bf16[2,128,512]{2,...) custom-call(s32[2,8]{1,0:T(2,128)} %bitcast.10, ...), custom_call_target="tpu_custom_call" | custom-call | flops 1000 | bytes 1000 | tf_op jit(solution)/shard_map/pick_head/pallas_call | solution.py:108
  3.0 1.3 %collective-permute-start = (bf16[2,128,512]{2,1,0:T(8,128)(2,1)S(1)}, bf16[2,128,512]{2,1,0:T(8,128)(2,1)S(1)}, u32[]{:S(2)}, u32[]{:S(2)}) collective-permute-start(bf16[2,128,512]{2,1,0:T(8,128)(2,1)S(1)} %get-tuple-element.29), channel_id=1, source_target_pairs={{0,12},{1,13},{2,14},{3,15},{4,8},{5,9},{6,10},{7,11},{8,0},{9,1},... | collective-permute-start | bytes 786440 | tf_op jit(solution)/shard_map/ppermute | solution.py:466
  4.3 0.9 collective-permute-start.1
  5.2 3.2 %collective-permute-start.2 = (bf16[2,128,512]{2,1,0:T(8,128)(2,1)S(1)}, bf16[2,128,512]{2,1,0:T(8,128)(2,1)S(1)}, u32[]{:S(2)}, u32[]{:S(2)}) collective-permute-start(bf16[2,128,512]{2,1,0:T(8,128)(2,1)S(1)} %get-tuple-element.31), channel_id=1, source_target_pairs={{0,6},{1,7},{2,4},{3,5},{4,2},{5,3},{6,0},{7,1},{8,14},{9,15},{10,... | collective-permute-start | bytes 786440 | tf_op jit(solution)/shard_map/ppermute | solution.py:466
  8.4 3.2 %collective-permute-start.4 = (bf16[2,128,512]{2,1,0:T(8,128)(2,1)S(1)}, bf16[2,128,512]{2,1,0:T(8,128)(2,1)S(1)}, u32[]{:S(2)}, u32[]{:S(2)}) collective-permute-start(bf16[2,128,512]{2,1,0:T(8,128)(2,1)S(1)} %get-tuple-element.33), channel_id=1, source_target_pairs={{0,14},{1,15},{2,12},{3,13},{4,10},{5,11},{6,8},{7,9},{8,2},{9,3},... | collective-permute-start | bytes 786440 | tf_op jit(solution)/shard_map/ppermute | solution.py:466
  11.6 3.2 %pick_tail.1 = (bf16[2,128,512]{2,1,0:T(8,128)(2,1)S(1)}, bf16[2,128,512]{2,1,0:T(8,128)(2,1)S(1)}, bf16[2,128,512]{2,1,0:T(8,128)(2,1)S(1)}, bf16[2,128,512]{2,...) custom-call(s32[2,8]{1,0:T(2,128)} %bitcast.11, ...), custom_call_target="tpu_custom_call" | custom-call | flops 1000 | bytes 1000 | tf_op jit(solution)/shard_map/pick_tail/pallas_call | solution.py:108
  14.8 5.7 %collective-permute-done.refs_0_ = bf16[2,128,512]{2,1,0:T(8,128)(2,1)S(1)} collective-permute-done((bf16[2,128,512]{2,1,0:T(8,128)(2,1)S(1)}, bf16[2,128,512]{2,1,0:T(8,128)(2,1)S(1)}, u32[]{:S(2)}, u32[]{:S(2)}) %collective-permute-start) | collective-permute-done | bytes 262176 | tf_op jit(solution)/shard_map/ppermute | solution.py:466
  20.5 1.2 %collective-permute-start.5 = (bf16[2,128,512]{2,1,0:T(8,128)(2,1)S(1)}, bf16[2,128,512]{2,1,0:T(8,128)(2,1)S(1)}, u32[]{:S(2)}, u32[]{:S(2)}) collective-permute-start(bf16[2,128,512]{2,1,0:T(8,128)(2,1)S(1)} %get-tuple-element.34), channel_id=1, source_target_pairs={{0,2},{1,3},{2,0},{3,1},{4,6},{5,7},{6,4},{7,5},{8,10},{9,11},{10,... | collective-permute-start | bytes 786440 | tf_op jit(solution)/shard_map/ppermute | solution.py:466
  21.8 4.4 %collective-permute-done.1.refs_1_ = bf16[2,128,512]{2,1,0:T(8,128)(2,1)S(1)} collective-permute-done((bf16[2,128,512]{2,1,0:T(8,128)(2,1)S(1)}, bf16[2,128,512]{2,1,0:T(8,128)(2,1)S(1)}, u32[]{:S(2)}, u32[]{:S(2)}) %collective-permute-start.1) | collective-permute-done | bytes 262176 | tf_op jit(solution)/shard_map/ppermute | solution.py:466
  26.2 2.8 %collective-permute-start.6 = (bf16[2,128,512]{2,1,0:T(8,128)(2,1)S(1)}, bf16[2,128,512]{2,1,0:T(8,128)(2,1)S(1)}, u32[]{:S(2)}, u32[]{:S(2)}) collective-permute-start(bf16[2,128,512]{2,1,0:T(8,128)(2,1)S(1)} %get-tuple-element.35), channel_id=1, source_target_pairs={{0,1},{1,0},{2,3},{3,2},{4,5},{5,4},{6,7},{7,6},{8,9},{9,8},{10,11... | collective-permute-start | bytes 786440 | tf_op jit(solution)/shard_map/ppermute | solution.py:466
  29.0 2.6 %collective-permute-start.7 = (bf16[2,128,512]{2,1,0:T(8,128)(2,1)S(1)}, bf16[2,128,512]{2,1,0:T(8,128)(2,1)S(1)}, u32[]{:S(2)}, u32[]{:S(2)}) collective-permute-start(bf16[2,128,512]{2,1,0:T(8,128)(2,1)S(1)} %get-tuple-element.36), channel_id=1, source_target_pairs={{0,4},{1,5},{2,6},{3,7},{4,0},{5,1},{6,2},{7,3},{8,12},{9,13},{10,... | collective-permute-start | bytes 786440 | tf_op jit(solution)/shard_map/ppermute | solution.py:466
  31.6 1.6 %collective-permute-done.3.refs_3_ = bf16[2,128,512]{2,1,0:T(8,128)(2,1)S(1)} collective-permute-done((bf16[2,128,512]{2,1,0:T(8,128)(2,1)S(1)}, bf16[2,128,512]{2,1,0:T(8,128)(2,1)S(1)}, u32[]{:S(2)}, u32[]{:S(2)}) %collective-permute-start.3) | collective-permute-done | bytes 262176 | tf_op jit(solution)/shard_map/ppermute | solution.py:466
  33.2 4.2 %collective-permute-done.4.refs_4_ = bf16[2,128,512]{2,1,0:T(8,128)(2,1)S(1)} collective-permute-done((bf16[2,128,512]{2,1,0:T(8,128)(2,1)S(1)}, bf16[2,128,512]{2,1,0:T(8,128)(2,1)S(1)}, u32[]{:S(2)}, u32[]{:S(2)}) %collective-permute-start.4) | collective-permute-done | bytes 262176 | tf_op jit(solution)/shard_map/ppermute | solution.py:466
  37.4 5.7 %collective-permute-start.9 = (bf16[2,128,512]{2,1,0:T(8,128)(2,1)S(1)}, bf16[2,128,512]{2,1,0:T(8,128)(2,1)S(1)}, u32[]{:S(2)}, u32[]{:S(2)}) collective-permute-start(bf16[2,128,512]{2,1,0:T(8,128)(2,1)S(1)} %get-tuple-element.38), channel_id=1, source_target_pairs={{0,5},{1,4},{2,7},{3,6},{4,1},{5,0},{6,3},{7,2},{8,13},{9,12},{10,... | collective-permute-start | bytes 786440 | tf_op jit(solution)/shard_map/ppermute | solution.py:466
  43.4 0.7 collective-permute-start.10
  44.1 0.9 factors.1
  45.4 2.0 %collective-permute-start.12 = (bf16[2,128,512]{2,1,0:T(8,128)(2,1)S(1)}, bf16[2,128,512]{2,1,0:T(8,128)(2,1)S(1)}, u32[]{:S(2)}, u32[]{:S(2)}) collective-permute-start(bf16[2,128,512]{2,1,0:T(8,128)(2,1)S(1)} %get-tuple-element.47), channel_id=1, source_target_pairs={{0,10},{1,11},{2,8},{3,9},{4,14},{5,15},{6,12},{7,13},{8,6},{9,7},... | collective-permute-start | bytes 786440 | tf_op jit(solution)/shard_map/ppermute | solution.py:466
  47.3 1.7 %collective-permute-done.8.refs_8_ = bf16[2,128,512]{2,1,0:T(8,128)(2,1)S(1)} collective-permute-done((bf16[2,128,512]{2,1,0:T(8,128)(2,1)S(1)}, bf16[2,128,512]{2,1,0:T(8,128)(2,1)S(1)}, u32[]{:S(2)}, u32[]{:S(2)}) %collective-permute-start.8) | collective-permute-done | bytes 262176 | tf_op jit(solution)/shard_map/ppermute | solution.py:466
  49.0 1.1 %collective-permute-start.13 = (bf16[2,128,512]{2,1,0:T(8,128)(2,1)S(1)}, bf16[2,128,512]{2,1,0:T(8,128)(2,1)S(1)}, u32[]{:S(2)}, u32[]{:S(2)}) collective-permute-start(bf16[2,128,512]{2,1,0:T(8,128)(2,1)S(1)} %get-tuple-element.48), channel_id=1, source_target_pairs={{0,9},{1,8},{2,11},{3,10},{4,13},{5,12},{6,15},{7,14},{8,5},{9,4},... | collective-permute-start | bytes 786440 | tf_op jit(solution)/shard_map/ppermute | solution.py:466
  50.1 22.1 %collective-permute-done.9.refs_9_ = bf16[2,128,512]{2,1,0:T(8,128)(2,1)S(1)} collective-permute-done((bf16[2,128,512]{2,1,0:T(8,128)(2,1)S(1)}, bf16[2,128,512]{2,1,0:T(8,128)(2,1)S(1)}, u32[]{:S(2)}, u32[]{:S(2)}) %collective-permute-start.9) | collective-permute-done | bytes 262176 | tf_op jit(solution)/shard_map/ppermute | solution.py:466
  72.2 5.6 %early_gram.1 = (bf16[768,2048]{1,0:T(8,128)(2,1)S(1)}, bf16[6,2,256,256]{3,2,1,0:T(8,128)(2,1)S(1)}, f32[4,8,128]{2,1,0:T(8,128)S(1)}) custom-call(bf16[2,128,512]{2,1,0:T(8,128)(2,1)S(1)} %collective-permute-done.refs_0_, bf16[2,128,512]{2,1,0:T(8,128)(2,1)S(1)} %collective-permute-done.1.refs_1_, bf16[2,128,512]{2,1,0:T(8,128)(2,1)S(1)} %collective-permute-done.2.refs_2_, ...), custom_call_target="tpu_custom_call" | custom-call | flops 49999998976 | bytes 1000 | tf_op jit(solution)/shard_map/early_gram/pallas_call | solution.py:193
  78.0 6.5 %all_to_all.5.other = bf16[2,6,2,256,256]{4,3,2,1,0:T(8,128)(2,1)S(1)} all-to-all(bf16[2,6,2,256,256]{4,3,2,1,0:T(8,128)(2,1)S(1)} %pad_maximum_fusion), channel_id=1, replica_groups=mesh['grp'=2,'tp'=8,'rb'=2] {'rb'}, dimensions={0} | all-to-all | bytes 6291456 | tf_op jit(solution)/shard_map/all_to_all | solution.py:472
  84.5 2.7 %early_cross.1.begun.refs_0_ = f32[2,8,128]{2,1,0:T(8,128)S(1)} custom-call(bf16[6,2,256,256]{3,2,1,0:T(8,128)(2,1)S(1)} %get-tuple-element.43.own, bf16[2,6,2,256,256]{4,3,2,1,0:T(8,128)(2,1)S(1)} %all_to_all.5.other, bf16[2,512,512]{2,1,0:T(8,128)(2,1)S(1)} %get-tuple-element.44.right, bf16[2,512,512]{2,1,0:T(8,128)(2,1)S(1)} %get-tuple-element.45.left), custom_call_target="tpu_custom_call" | custom-call | flops 1000 | bytes 1000 | tf_op jit(solution)/shard_map/early_cross/pallas_call | solution.py:385
  87.3 1.4 %late_begin.1.partial = f32[4,2,256,256]{3,2,1,0:T(8,128)S(1)} custom-call(bf16[768,2048]{1,0:T(8,128)(2,1)S(1)} %get-tuple-element.42.flat, f32[2,8,128]{2,1,0:T(8,128)S(1)} %early_cross.1.begun.refs_0_, bf16[2,128,512]{2,1,0:T(8,128)(2,1)S(1)} %collective-permute-done.11.refs_0_, bf16[2,128,512]{2,1,0:T(8,128)(2,1)S(1)} %collective-permute-done.12.refs_1_), custom_call_target="tpu_custom_call" | custom-call | flops 1000 | bytes 1000 | tf_op jit(solution)/shard_map/late_begin/pallas_call | solution.py:239
  88.6 2.5 %collective-permute-done.13.refs_0_ = bf16[2,128,512]{2,1,0:T(8,128)(2,1)S(1)} collective-permute-done((bf16[2,128,512]{2,1,0:T(8,128)(2,1)S(1)}, bf16[2,128,512]{2,1,0:T(8,128)(2,1)S(1)}, u32[]{:S(2)}, u32[]{:S(2)}) %collective-permute-start.13) | collective-permute-done | bytes 262176 | tf_op jit(solution)/shard_map/ppermute | solution.py:466
  91.2 5.2 %collective-permute-done.14.refs_1_ = bf16[2,128,512]{2,1,0:T(8,128)(2,1)S(1)} collective-permute-done((bf16[2,128,512]{2,1,0:T(8,128)(2,1)S(1)}, bf16[2,128,512]{2,1,0:T(8,128)(2,1)S(1)}, u32[]{:S(2)}, u32[]{:S(2)}) %collective-permute-start.14) | collective-permute-done | bytes 262176 | tf_op jit(solution)/shard_map/ppermute | solution.py:466
  96.3 0.8 late_rows.1
  97.2 0.8 late_rest.1.rest.own
  98.0 0.6 collective-permute-start.15
  99.1 1.3 %late_cross.1.carried = f32[2,8,128]{2,1,0:T(8,128)S(1)} custom-call(bf16[2,2,256,256]{3,2,1,0:T(8,128)(2,1)S(1)} %get-tuple-element.52.own, bf16[2,2,256,256]{3,2,1,0:T(8,128)(2,1)S(1)} %collective-permute-done.16.other, bf16[2,512,512]{2,1,0:T(8,128)(2,1)S(1)} %get-tuple-element.44.right, bf16[2,512,512]{2,1,0:T(8,128)(2,1)S(1)} %get-tuple-element.45.left, ...), custom_call_target="tpu_custom_call" | custom-call | flops 1000 | bytes 1000 | tf_op jit(solution)/shard_map/late_cross/pallas_call | solution.py:385
  100.4 1.0 last_cross.1.mine
  102.7 0.7 final.1
  (22 shorter events, 2.2 us)
Async XLA Ops:
  3.0 17.6 %collective-permute-start = (bf16[2,128,512]{2,1,0:T(8,128)(2,1)S(1)}, bf16[2,128,512]{2,1,0:T(8,128)(2,1)S(1)}, u32[]{:S(2)}, u32[]{:S(2)}) collective-permute-start(bf16[2,128,512]{2,1,0:T(8,128)(2,1)S(1)} %get-tuple-element.29), channel_id=1, source_target_pairs={{0,12},{1,13},{2,14},{3,15},{4,8},{5,9},{6,10},{7,11},{8,0},{9,1},... | collective-permute-start | bytes 786440 | tf_op jit(solution)/shard_map/ppermute | solution.py:466
  4.3 21.8 %collective-permute-start.1 = (bf16[2,128,512]{2,1,0:T(8,128)(2,1)S(1)}, bf16[2,128,512]{2,1,0:T(8,128)(2,1)S(1)}, u32[]{:S(2)}, u32[]{:S(2)}) collective-permute-start(bf16[2,128,512]{2,1,0:T(8,128)(2,1)S(1)} %get-tuple-element.30), channel_id=1, source_target_pairs={{0,13},{1,12},{2,15},{3,14},{4,9},{5,8},{6,11},{7,10},{8,1},{9,0},... | collective-permute-start | bytes 786440 | tf_op jit(solution)/shard_map/ppermute | solution.py:466
  5.2 23.8 %collective-permute-start.2 = (bf16[2,128,512]{2,1,0:T(8,128)(2,1)S(1)}, bf16[2,128,512]{2,1,0:T(8,128)(2,1)S(1)}, u32[]{:S(2)}, u32[]{:S(2)}) collective-permute-start(bf16[2,128,512]{2,1,0:T(8,128)(2,1)S(1)} %get-tuple-element.31), channel_id=1, source_target_pairs={{0,6},{1,7},{2,4},{3,5},{4,2},{5,3},{6,0},{7,1},{8,14},{9,15},{10,... | collective-permute-start | bytes 786440 | tf_op jit(solution)/shard_map/ppermute | solution.py:466
  8.4 24.8 %collective-permute-start.3 = (bf16[2,128,512]{2,1,0:T(8,128)(2,1)S(1)}, bf16[2,128,512]{2,1,0:T(8,128)(2,1)S(1)}, u32[]{:S(2)}, u32[]{:S(2)}) collective-permute-start(bf16[2,128,512]{2,1,0:T(8,128)(2,1)S(1)} %get-tuple-element.32), channel_id=1, source_target_pairs={{0,7},{1,6},{2,5},{3,4},{4,3},{5,2},{6,1},{7,0},{8,15},{9,14},{10,... | collective-permute-start | bytes 786440 | tf_op jit(solution)/shard_map/ppermute | solution.py:466
  8.4 35.7 %copy-start = (bf16[7,2,256,256]{3,2,1,0:T(8,128)(2,1)S(1)}, bf16[7,2,256,256]{3,2,1,0:T(8,128)(2,1)}, u32[]{:S(2)}) copy-start(bf16[7,2,256,256]{3,2,1,0:T(8,128)(2,1)} %elems.1) | copy-start | bytes 5505028
  8.4 35.7 %copy-start.1 = (s32[1,2,2]{2,1,0:T(2,128)S(1)}, s32[1,2,2]{2,1,0:T(2,128)}, u32[]{:S(2)}) copy-start(s32[1,2,2]{2,1,0:T(2,128)} %diag_mom.1) | copy-start | bytes 52
  8.4 29.0 %collective-permute-start.4 = (bf16[2,128,512]{2,1,0:T(8,128)(2,1)S(1)}, bf16[2,128,512]{2,1,0:T(8,128)(2,1)S(1)}, u32[]{:S(2)}, u32[]{:S(2)}) collective-permute-start(bf16[2,128,512]{2,1,0:T(8,128)(2,1)S(1)} %get-tuple-element.33), channel_id=1, source_target_pairs={{0,14},{1,15},{2,12},{3,13},{4,10},{5,11},{6,8},{7,9},{8,2},{9,3},... | collective-permute-start | bytes 786440 | tf_op jit(solution)/shard_map/ppermute | solution.py:466
  20.5 22.9 %collective-permute-start.5 = (bf16[2,128,512]{2,1,0:T(8,128)(2,1)S(1)}, bf16[2,128,512]{2,1,0:T(8,128)(2,1)S(1)}, u32[]{:S(2)}, u32[]{:S(2)}) collective-permute-start(bf16[2,128,512]{2,1,0:T(8,128)(2,1)S(1)} %get-tuple-element.34), channel_id=1, source_target_pairs={{0,2},{1,3},{2,0},{3,1},{4,6},{5,7},{6,4},{7,5},{8,10},{9,11},{10,... | collective-permute-start | bytes 786440 | tf_op jit(solution)/shard_map/ppermute | solution.py:466
  26.2 18.9 %collective-permute-start.6 = (bf16[2,128,512]{2,1,0:T(8,128)(2,1)S(1)}, bf16[2,128,512]{2,1,0:T(8,128)(2,1)S(1)}, u32[]{:S(2)}, u32[]{:S(2)}) collective-permute-start(bf16[2,128,512]{2,1,0:T(8,128)(2,1)S(1)} %get-tuple-element.35), channel_id=1, source_target_pairs={{0,1},{1,0},{2,3},{3,2},{4,5},{5,4},{6,7},{7,6},{8,9},{9,8},{10,11... | collective-permute-start | bytes 786440 | tf_op jit(solution)/shard_map/ppermute | solution.py:466
  29.0 16.4 %collective-permute-start.7 = (bf16[2,128,512]{2,1,0:T(8,128)(2,1)S(1)}, bf16[2,128,512]{2,1,0:T(8,128)(2,1)S(1)}, u32[]{:S(2)}, u32[]{:S(2)}) collective-permute-start(bf16[2,128,512]{2,1,0:T(8,128)(2,1)S(1)} %get-tuple-element.36), channel_id=1, source_target_pairs={{0,4},{1,5},{2,6},{3,7},{4,0},{5,1},{6,2},{7,3},{8,12},{9,13},{10,... | collective-permute-start | bytes 786440 | tf_op jit(solution)/shard_map/ppermute | solution.py:466
  33.2 15.8 %collective-permute-start.8 = (bf16[2,128,512]{2,1,0:T(8,128)(2,1)S(1)}, bf16[2,128,512]{2,1,0:T(8,128)(2,1)S(1)}, u32[]{:S(2)}, u32[]{:S(2)}) collective-permute-start(bf16[2,128,512]{2,1,0:T(8,128)(2,1)S(1)} %get-tuple-element.37), channel_id=1, source_target_pairs={{0,15},{1,14},{2,13},{3,12},{4,11},{5,10},{6,9},{7,8},{8,3},{9,2},... | collective-permute-start | bytes 786440 | tf_op jit(solution)/shard_map/ppermute | solution.py:466
  37.4 34.8 %collective-permute-start.9 = (bf16[2,128,512]{2,1,0:T(8,128)(2,1)S(1)}, bf16[2,128,512]{2,1,0:T(8,128)(2,1)S(1)}, u32[]{:S(2)}, u32[]{:S(2)}) collective-permute-start(bf16[2,128,512]{2,1,0:T(8,128)(2,1)S(1)} %get-tuple-element.38), channel_id=1, source_target_pairs={{0,5},{1,4},{2,7},{3,6},{4,1},{5,0},{6,3},{7,2},{8,13},{9,12},{10,... | collective-permute-start | bytes 786440 | tf_op jit(solution)/shard_map/ppermute | solution.py:466
  43.4 28.7 %collective-permute-start.10 = (bf16[2,128,512]{2,1,0:T(8,128)(2,1)S(1)}, bf16[2,128,512]{2,1,0:T(8,128)(2,1)S(1)}, u32[]{:S(2)}, u32[]{:S(2)}) collective-permute-start(bf16[2,128,512]{2,1,0:T(8,128)(2,1)S(1)} %get-tuple-element.39), channel_id=1, source_target_pairs={{0,3},{1,2},{2,1},{3,0},{4,7},{5,6},{6,5},{7,4},{8,11},{9,10},{10,... | collective-permute-start | bytes 786440 | tf_op jit(solution)/shard_map/ppermute | solution.py:466
  45.1 42.2 %collective-permute-start.11 = (bf16[2,128,512]{2,1,0:T(8,128)(2,1)S(1)}, bf16[2,128,512]{2,1,0:T(8,128)(2,1)S(1)}, u32[]{:S(2)}, u32[]{:S(2)}) collective-permute-start(bf16[2,128,512]{2,1,0:T(8,128)(2,1)S(1)} %get-tuple-element.46), channel_id=1, source_target_pairs={{0,8},{1,9},{2,10},{3,11},{4,12},{5,13},{6,14},{7,15},{8,4},{9,5},... | collective-permute-start | bytes 786440 | tf_op jit(solution)/shard_map/ppermute | solution.py:466
  45.4 41.9 %collective-permute-start.12 = (bf16[2,128,512]{2,1,0:T(8,128)(2,1)S(1)}, bf16[2,128,512]{2,1,0:T(8,128)(2,1)S(1)}, u32[]{:S(2)}, u32[]{:S(2)}) collective-permute-start(bf16[2,128,512]{2,1,0:T(8,128)(2,1)S(1)} %get-tuple-element.47), channel_id=1, source_target_pairs={{0,10},{1,11},{2,8},{3,9},{4,14},{5,15},{6,12},{7,13},{8,6},{9,7},... | collective-permute-start | bytes 786440 | tf_op jit(solution)/shard_map/ppermute | solution.py:466
  49.0 42.2 %collective-permute-start.13 = (bf16[2,128,512]{2,1,0:T(8,128)(2,1)S(1)}, bf16[2,128,512]{2,1,0:T(8,128)(2,1)S(1)}, u32[]{:S(2)}, u32[]{:S(2)}) collective-permute-start(bf16[2,128,512]{2,1,0:T(8,128)(2,1)S(1)} %get-tuple-element.48), channel_id=1, source_target_pairs={{0,9},{1,8},{2,11},{3,10},{4,13},{5,12},{6,15},{7,14},{8,5},{9,4},... | collective-permute-start | bytes 786440 | tf_op jit(solution)/shard_map/ppermute | solution.py:466
  72.2 24.2 %collective-permute-start.14 = (bf16[2,128,512]{2,1,0:T(8,128)(2,1)S(1)}, bf16[2,128,512]{2,1,0:T(8,128)(2,1)S(1)}, u32[]{:S(2)}, u32[]{:S(2)}) collective-permute-start(bf16[2,128,512]{2,1,0:T(8,128)(2,1)S(1)} %get-tuple-element.49), channel_id=1, source_target_pairs={{0,11},{1,10},{2,9},{3,8},{4,15},{5,14},{6,13},{7,12},{8,7},{9,6},... | collective-permute-start | bytes 786440 | tf_op jit(solution)/shard_map/ppermute | solution.py:466
  97.1 2.0 %collective-permute-start.16 = (bf16[2,2,256,256]{3,2,1,0:T(8,128)(2,1)S(1)}, bf16[2,2,256,256]{3,2,1,0:T(8,128)(2,1)S(1)}, u32[]{:S(2)}, u32[]{:S(2)}) collective-permute-start(bf16[2,2,256,256]{3,2,1,0:T(8,128)(2,1)S(1)} %get-tuple-element.52.own), channel_id=1, source_target_pairs={{0,1},{1,0},{2,3},{3,2},{4,5},{5,4},{6,7},{7,6},{8,9},{9,8},{10,11... | collective-permute-start | bytes 1572872 | tf_op jit(solution)/shard_map/ppermute | solution.py:480
  98.0 2.4 %collective-permute-start.15 = (bf16[2,2,256,256]{3,2,1,0:T(8,128)(2,1)S(1)}, bf16[2,2,256,256]{3,2,1,0:T(8,128)(2,1)S(1)}, u32[]{:S(2)}, u32[]{:S(2)}) collective-permute-start(bf16[2,2,256,256]{3,2,1,0:T(8,128)(2,1)S(1)} %late_rest.1.rest.own), channel_id=1, source_target_pairs={{0,1},{1,0},{2,3},{3,2},{4,5},{5,4},{6,7},{7,6},{8,9},{9,8},{10,11... | collective-permute-start | bytes 1572872 | tf_op jit(solution)/shard_map/ppermute | solution.py:482
  101.4 1.3 %collective-permute-start.17 = (f32[6,8,128]{2,1,0:T(8,128)S(1)}, f32[6,8,128]{2,1,0:T(8,128)S(1)}, u32[]{:S(2)}, u32[]{:S(2)}) collective-permute-start(f32[6,8,128]{2,1,0:T(8,128)S(1)} %last_cross.1.mine), channel_id=1, source_target_pairs={{0,1},{1,0},{2,3},{3,2},{4,5},{5,4},{6,7},{7,6},{8,9},{9,8},{10,11... | collective-permute-start | bytes 73736 | tf_op jit(solution)/shard_map/ppermute | solution.py:486

commit v2 on v1

--- a/solution.py
+++ b/solution.py
@@ -58,7 +58,7 @@
     own, other = (0, 0), [(0, side) for side in range(1, rb_count)]
     step, part = len(long) // 4, len(rest) // 2
     head = long[: 2 * step] + near[: 2 * step] + long[2 * step : 3 * step]
-    tail = rest[:part] + other + near[2 * step : 3 * step] + long[3 * step :] + near[3 * step :] + rest[part:]
+    tail = rest[:part] + other + near[2 * step : 3 * step] + long[3 * step :] + rest[part:] + near[3 * step :]
     return head, tail, late, [own]
 
 

time: 104 us -> 104 us (level)
  waiting for transfers between devices: 48.3 us -> 27.9 us
  blocking collectives: 6.49 us -> 25.6 us
  starting transfers between devices: 25.8 us -> 27.2 us
    ppermute x15, waiting for transfers between devices: 47.7 us -> 27.2 us  [send(): return lax.ppermute(picked[key], ('tp', 'rb'), pairs)]
    all_to_all x1, blocking collectives: 6.49 us -> 25.6 us  [shards(): early_both = lax.all_to_all(jnp.stack([early] * rb_count), 'rb', 0, 0)]
    ppermute x15, starting transfers between devices: 25 us -> 26.3 us  [send(): return lax.ppermute(picked[key], ('tp', 'rb'), pairs)]
  transfers between devices with their start and end apart: 18 -> 18, of which waited for: 11 -> 10; matrix products, arithmetic and copies ran while one was open for 0% -> 0% of each run, Pallas kernels for 16% -> 16%
where the time goes in v2:
time: 104 us; the launch traced here: 103 us
  waiting for transfers between devices  27.9 us (27%)
  starting transfers between devices  27.2 us (26%)
  blocking collectives  25.6 us (25%)
  Pallas kernels  21.7 us (21%)
    ppermute x15, waiting for transfers between devices, send(): return lax.ppermute(picked[key], ('tp', 'rb'), pairs)  27.2 us
    ppermute x15, starting transfers between devices, send(): return lax.ppermute(picked[key], ('tp', 'rb'), pairs)  26.3 us
    all_to_all x1, blocking collectives, shards(): early_both = lax.all_to_all(jnp.stack([early] * rb_count), 'rb', 0, 0)  25.6 us
    pallas_call x2, Pallas kernels, pick(): pl.pallas_call(functools.partial(pick_kernel, keys), out_shape=[jax.Shape...  6.19 us
    pallas_call x1, Pallas kernels, early_gram(): pl.pallas_call(functools.partial(early_kernel, eig, keys, rb_count, block...  5.57 us
    pallas_call x2, Pallas kernels, cross_traces(): pl.pallas_call(functools.partial(cross_kernel, offs), out_shape=sums_shap...  4.02 us
  transfers between devices with their start and end apart: 18, of which 10 were waited for; matrix products, arithmetic and copies ran while one was open for 0% of the time, Pallas kernels for 16%

profile of v2, /device:TPU:11, one launch (start us, length us, event | category | flops | bytes accessed | tf_op | source)
XLA Modules:
  0.0 103.4 jit_solution(15484871042797102343)
XLA Ops:
  0.0 3.0 %pick_head.1 = (bf16[2,128,512]{2,1,0:T(8,128)(2,1)S(1)}, bf16[2,128,512]{2,1,0:T(8,128)(2,1)S(1)}, bf16[2,128,512]{2,1,0:T(8,128)(2,1)S(1)}, bf16[2,128,512]{2,...) custom-call(s32[2,8]{1,0:T(2,128)} %bitcast.10, ...), custom_call_target="tpu_custom_call" | custom-call | flops 1000 | bytes 1000 | tf_op jit(solution)/shard_map/pick_head/pallas_call | solution.py:108
  3.0 1.4 %collective-permute-start = (bf16[2,128,512]{2,1,0:T(8,128)(2,1)S(1)}, bf16[2,128,512]{2,1,0:T(8,128)(2,1)S(1)}, u32[]{:S(2)}, u32[]{:S(2)}) collective-permute-start(bf16[2,128,512]{2,1,0:T(8,128)(2,1)S(1)} %get-tuple-element.29), channel_id=1, source_target_pairs={{0,12},{1,13},{2,14},{3,15},{4,8},{5,9},{6,10},{7,11},{8,0},{9,1},... | collective-permute-start | bytes 786440 | tf_op jit(solution)/shard_map/ppermute | solution.py:466
  4.3 0.9 collective-permute-start.1
  5.2 3.2 %collective-permute-start.2 = (bf16[2,128,512]{2,1,0:T(8,128)(2,1)S(1)}, bf16[2,128,512]{2,1,0:T(8,128)(2,1)S(1)}, u32[]{:S(2)}, u32[]{:S(2)}) collective-permute-start(bf16[2,128,512]{2,1,0:T(8,128)(2,1)S(1)} %get-tuple-element.31), channel_id=1, source_target_pairs={{0,6},{1,7},{2,4},{3,5},{4,2},{5,3},{6,0},{7,1},{8,14},{9,15},{10,... | collective-permute-start | bytes 786440 | tf_op jit(solution)/shard_map/ppermute | solution.py:466
  8.4 3.2 %collective-permute-start.4 = (bf16[2,128,512]{2,1,0:T(8,128)(2,1)S(1)}, bf16[2,128,512]{2,1,0:T(8,128)(2,1)S(1)}, u32[]{:S(2)}, u32[]{:S(2)}) collective-permute-start(bf16[2,128,512]{2,1,0:T(8,128)(2,1)S(1)} %get-tuple-element.33), channel_id=1, source_target_pairs={{0,14},{1,15},{2,12},{3,13},{4,10},{5,11},{6,8},{7,9},{8,2},{9,3},... | collective-permute-start | bytes 786440 | tf_op jit(solution)/shard_map/ppermute | solution.py:466
  11.6 3.2 %pick_tail.1 = (bf16[2,128,512]{2,1,0:T(8,128)(2,1)S(1)}, bf16[2,128,512]{2,1,0:T(8,128)(2,1)S(1)}, bf16[2,128,512]{2,1,0:T(8,128)(2,1)S(1)}, bf16[2,128,512]{2,...) custom-call(s32[2,8]{1,0:T(2,128)} %bitcast.11, ...), custom_call_target="tpu_custom_call" | custom-call | flops 1000 | bytes 1000 | tf_op jit(solution)/shard_map/pick_tail/pallas_call | solution.py:108
  14.8 5.7 %collective-permute-done.refs_0_ = bf16[2,128,512]{2,1,0:T(8,128)(2,1)S(1)} collective-permute-done((bf16[2,128,512]{2,1,0:T(8,128)(2,1)S(1)}, bf16[2,128,512]{2,1,0:T(8,128)(2,1)S(1)}, u32[]{:S(2)}, u32[]{:S(2)}) %collective-permute-start) | collective-permute-done | bytes 262176 | tf_op jit(solution)/shard_map/ppermute | solution.py:466
  20.6 1.2 %collective-permute-start.5 = (bf16[2,128,512]{2,1,0:T(8,128)(2,1)S(1)}, bf16[2,128,512]{2,1,0:T(8,128)(2,1)S(1)}, u32[]{:S(2)}, u32[]{:S(2)}) collective-permute-start(bf16[2,128,512]{2,1,0:T(8,128)(2,1)S(1)} %get-tuple-element.34), channel_id=1, source_target_pairs={{0,2},{1,3},{2,0},{3,1},{4,6},{5,7},{6,4},{7,5},{8,10},{9,11},{10,... | collective-permute-start | bytes 786440 | tf_op jit(solution)/shard_map/ppermute | solution.py:466
  21.8 4.4 %collective-permute-done.1.refs_1_ = bf16[2,128,512]{2,1,0:T(8,128)(2,1)S(1)} collective-permute-done((bf16[2,128,512]{2,1,0:T(8,128)(2,1)S(1)}, bf16[2,128,512]{2,1,0:T(8,128)(2,1)S(1)}, u32[]{:S(2)}, u32[]{:S(2)}) %collective-permute-start.1) | collective-permute-done | bytes 262176 | tf_op jit(solution)/shard_map/ppermute | solution.py:466
  26.2 2.8 %collective-permute-start.6 = (bf16[2,128,512]{2,1,0:T(8,128)(2,1)S(1)}, bf16[2,128,512]{2,1,0:T(8,128)(2,1)S(1)}, u32[]{:S(2)}, u32[]{:S(2)}) collective-permute-start(bf16[2,128,512]{2,1,0:T(8,128)(2,1)S(1)} %get-tuple-element.35), channel_id=1, source_target_pairs={{0,1},{1,0},{2,3},{3,2},{4,5},{5,4},{6,7},{7,6},{8,9},{9,8},{10,11... | collective-permute-start | bytes 786440 | tf_op jit(solution)/shard_map/ppermute | solution.py:466
  29.0 2.6 %collective-permute-start.7 = (bf16[2,128,512]{2,1,0:T(8,128)(2,1)S(1)}, bf16[2,128,512]{2,1,0:T(8,128)(2,1)S(1)}, u32[]{:S(2)}, u32[]{:S(2)}) collective-permute-start(bf16[2,128,512]{2,1,0:T(8,128)(2,1)S(1)} %get-tuple-element.36), channel_id=1, source_target_pairs={{0,4},{1,5},{2,6},{3,7},{4,0},{5,1},{6,2},{7,3},{8,12},{9,13},{10,... | collective-permute-start | bytes 786440 | tf_op jit(solution)/shard_map/ppermute | solution.py:466
  31.6 1.6 %collective-permute-done.3.refs_3_ = bf16[2,128,512]{2,1,0:T(8,128)(2,1)S(1)} collective-permute-done((bf16[2,128,512]{2,1,0:T(8,128)(2,1)S(1)}, bf16[2,128,512]{2,1,0:T(8,128)(2,1)S(1)}, u32[]{:S(2)}, u32[]{:S(2)}) %collective-permute-start.3) | collective-permute-done | bytes 262176 | tf_op jit(solution)/shard_map/ppermute | solution.py:466
  33.2 4.2 %collective-permute-done.4.refs_4_ = bf16[2,128,512]{2,1,0:T(8,128)(2,1)S(1)} collective-permute-done((bf16[2,128,512]{2,1,0:T(8,128)(2,1)S(1)}, bf16[2,128,512]{2,1,0:T(8,128)(2,1)S(1)}, u32[]{:S(2)}, u32[]{:S(2)}) %collective-permute-start.4) | collective-permute-done | bytes 262176 | tf_op jit(solution)/shard_map/ppermute | solution.py:466
  37.4 3.9 %collective-permute-start.9 = (bf16[2,128,512]{2,1,0:T(8,128)(2,1)S(1)}, bf16[2,128,512]{2,1,0:T(8,128)(2,1)S(1)}, u32[]{:S(2)}, u32[]{:S(2)}) collective-permute-start(bf16[2,128,512]{2,1,0:T(8,128)(2,1)S(1)} %get-tuple-element.38), channel_id=1, source_target_pairs={{0,3},{1,2},{2,1},{3,0},{4,7},{5,6},{6,5},{7,4},{8,11},{9,10},{10,... | collective-permute-start | bytes 786440 | tf_op jit(solution)/shard_map/ppermute | solution.py:466
  41.4 2.1 %collective-permute-done.5.refs_5_ = bf16[2,128,512]{2,1,0:T(8,128)(2,1)S(1)} collective-permute-done((bf16[2,128,512]{2,1,0:T(8,128)(2,1)S(1)}, bf16[2,128,512]{2,1,0:T(8,128)(2,1)S(1)}, u32[]{:S(2)}, u32[]{:S(2)}) %collective-permute-start.5) | collective-permute-done | bytes 262176 | tf_op jit(solution)/shard_map/ppermute | solution.py:466
  43.4 0.9 factors.1
  44.4 1.0 collective-permute-start.11
  45.4 3.0 %collective-permute-start.12 = (bf16[2,128,512]{2,1,0:T(8,128)(2,1)S(1)}, bf16[2,128,512]{2,1,0:T(8,128)(2,1)S(1)}, u32[]{:S(2)}, u32[]{:S(2)}) collective-permute-start(bf16[2,128,512]{2,1,0:T(8,128)(2,1)S(1)} %get-tuple-element.47), channel_id=1, source_target_pairs={{0,10},{1,11},{2,8},{3,9},{4,14},{5,15},{6,12},{7,13},{8,6},{9,7},... | collective-permute-start | bytes 786440 | tf_op jit(solution)/shard_map/ppermute | solution.py:466
  48.4 0.6 collective-permute-done.8.refs_8_
  49.0 0.8 collective-permute-start.13
  49.8 4.0 %collective-permute-done.9.refs_9_ = bf16[2,128,512]{2,1,0:T(8,128)(2,1)S(1)} collective-permute-done((bf16[2,128,512]{2,1,0:T(8,128)(2,1)S(1)}, bf16[2,128,512]{2,1,0:T(8,128)(2,1)S(1)}, u32[]{:S(2)}, u32[]{:S(2)}) %collective-permute-start.9) | collective-permute-done | bytes 262176 | tf_op jit(solution)/shard_map/ppermute | solution.py:466
  53.8 2.3 %collective-permute-start.14 = (bf16[2,128,512]{2,1,0:T(8,128)(2,1)S(1)}, bf16[2,128,512]{2,1,0:T(8,128)(2,1)S(1)}, u32[]{:S(2)}, u32[]{:S(2)}) collective-permute-start(bf16[2,128,512]{2,1,0:T(8,128)(2,1)S(1)} %get-tuple-element.49), channel_id=1, source_target_pairs={{0,11},{1,10},{2,9},{3,8},{4,15},{5,14},{6,13},{7,12},{8,7},{9,6},... | collective-permute-start | bytes 786440 | tf_op jit(solution)/shard_map/ppermute | solution.py:466
  56.1 5.6 %early_gram.1 = (bf16[768,2048]{1,0:T(8,128)(2,1)S(1)}, bf16[6,2,256,256]{3,2,1,0:T(8,128)(2,1)S(1)}, f32[4,8,128]{2,1,0:T(8,128)S(1)}) custom-call(bf16[2,128,512]{2,1,0:T(8,128)(2,1)S(1)} %collective-permute-done.refs_0_, bf16[2,128,512]{2,1,0:T(8,128)(2,1)S(1)} %collective-permute-done.1.refs_1_, bf16[2,128,512]{2,1,0:T(8,128)(2,1)S(1)} %collective-permute-done.2.refs_2_, ...), custom_call_target="tpu_custom_call" | custom-call | flops 49999998976 | bytes 1000 | tf_op jit(solution)/shard_map/early_gram/pallas_call | solution.py:193
  62.0 25.6 %all_to_all.5.other = bf16[2,6,2,256,256]{4,3,2,1,0:T(8,128)(2,1)S(1)} all-to-all(bf16[2,6,2,256,256]{4,3,2,1,0:T(8,128)(2,1)S(1)} %pad_maximum_fusion), channel_id=1, replica_groups=mesh['grp'=2,'tp'=8,'rb'=2] {'rb'}, dimensions={0} | all-to-all | bytes 6291456 | tf_op jit(solution)/shard_map/all_to_all | solution.py:472
  87.6 2.7 %early_cross.1.begun.refs_0_ = f32[2,8,128]{2,1,0:T(8,128)S(1)} custom-call(bf16[6,2,256,256]{3,2,1,0:T(8,128)(2,1)S(1)} %get-tuple-element.43.own, bf16[2,6,2,256,256]{4,3,2,1,0:T(8,128)(2,1)S(1)} %all_to_all.5.other, bf16[2,512,512]{2,1,0:T(8,128)(2,1)S(1)} %get-tuple-element.44.right, bf16[2,512,512]{2,1,0:T(8,128)(2,1)S(1)} %get-tuple-element.45.left), custom_call_target="tpu_custom_call" | custom-call | flops 1000 | bytes 1000 | tf_op jit(solution)/shard_map/early_cross/pallas_call | solution.py:385
  90.3 1.4 %late_begin.1.partial = f32[4,2,256,256]{3,2,1,0:T(8,128)S(1)} custom-call(bf16[768,2048]{1,0:T(8,128)(2,1)S(1)} %get-tuple-element.42.flat, f32[2,8,128]{2,1,0:T(8,128)S(1)} %early_cross.1.begun.refs_0_, bf16[2,128,512]{2,1,0:T(8,128)(2,1)S(1)} %collective-permute-done.11.refs_0_, bf16[2,128,512]{2,1,0:T(8,128)(2,1)S(1)} %collective-permute-done.12.refs_1_), custom_call_target="tpu_custom_call" | custom-call | flops 1000 | bytes 1000 | tf_op jit(solution)/shard_map/late_begin/pallas_call | solution.py:239
  91.7 4.6 %collective-permute-done.14.refs_1_ = bf16[2,128,512]{2,1,0:T(8,128)(2,1)S(1)} collective-permute-done((bf16[2,128,512]{2,1,0:T(8,128)(2,1)S(1)}, bf16[2,128,512]{2,1,0:T(8,128)(2,1)S(1)}, u32[]{:S(2)}, u32[]{:S(2)}) %collective-permute-start.14) | collective-permute-done | bytes 262176 | tf_op jit(solution)/shard_map/ppermute | solution.py:466
  96.3 0.8 late_rows.1
  97.2 0.8 late_rest.1.rest.own
  99.1 1.3 %late_cross.1.carried = f32[2,8,128]{2,1,0:T(8,128)S(1)} custom-call(bf16[2,2,256,256]{3,2,1,0:T(8,128)(2,1)S(1)} %get-tuple-element.52.own, bf16[2,2,256,256]{3,2,1,0:T(8,128)(2,1)S(1)} %collective-permute-done.16.other, bf16[2,512,512]{2,1,0:T(8,128)(2,1)S(1)} %get-tuple-element.44.right, bf16[2,512,512]{2,1,0:T(8,128)(2,1)S(1)} %get-tuple-element.45.left, ...), custom_call_target="tpu_custom_call" | custom-call | flops 1000 | bytes 1000 | tf_op jit(solution)/shard_map/late_cross/pallas_call | solution.py:385
  100.4 1.0 last_cross.1.mine
  102.7 0.7 final.1
  (22 shorter events, 2.1 us)
Async XLA Ops:
  3.0 17.6 %collective-permute-start = (bf16[2,128,512]{2,1,0:T(8,128)(2,1)S(1)}, bf16[2,128,512]{2,1,0:T(8,128)(2,1)S(1)}, u32[]{:S(2)}, u32[]{:S(2)}) collective-permute-start(bf16[2,128,512]{2,1,0:T(8,128)(2,1)S(1)} %get-tuple-element.29), channel_id=1, source_target_pairs={{0,12},{1,13},{2,14},{3,15},{4,8},{5,9},{6,10},{7,11},{8,0},{9,1},... | collective-permute-start | bytes 786440 | tf_op jit(solution)/shard_map/ppermute | solution.py:466
  4.3 21.8 %collective-permute-start.1 = (bf16[2,128,512]{2,1,0:T(8,128)(2,1)S(1)}, bf16[2,128,512]{2,1,0:T(8,128)(2,1)S(1)}, u32[]{:S(2)}, u32[]{:S(2)}) collective-permute-start(bf16[2,128,512]{2,1,0:T(8,128)(2,1)S(1)} %get-tuple-element.30), channel_id=1, source_target_pairs={{0,13},{1,12},{2,15},{3,14},{4,9},{5,8},{6,11},{7,10},{8,1},{9,0},... | collective-permute-start | bytes 786440 | tf_op jit(solution)/shard_map/ppermute | solution.py:466
  5.2 23.7 %collective-permute-start.2 = (bf16[2,128,512]{2,1,0:T(8,128)(2,1)S(1)}, bf16[2,128,512]{2,1,0:T(8,128)(2,1)S(1)}, u32[]{:S(2)}, u32[]{:S(2)}) collective-permute-start(bf16[2,128,512]{2,1,0:T(8,128)(2,1)S(1)} %get-tuple-element.31), channel_id=1, source_target_pairs={{0,6},{1,7},{2,4},{3,5},{4,2},{5,3},{6,0},{7,1},{8,14},{9,15},{10,... | collective-permute-start | bytes 786440 | tf_op jit(solution)/shard_map/ppermute | solution.py:466
  8.4 24.8 %collective-permute-start.3 = (bf16[2,128,512]{2,1,0:T(8,128)(2,1)S(1)}, bf16[2,128,512]{2,1,0:T(8,128)(2,1)S(1)}, u32[]{:S(2)}, u32[]{:S(2)}) collective-permute-start(bf16[2,128,512]{2,1,0:T(8,128)(2,1)S(1)} %get-tuple-element.32), channel_id=1, source_target_pairs={{0,7},{1,6},{2,5},{3,4},{4,3},{5,2},{6,1},{7,0},{8,15},{9,14},{10,... | collective-permute-start | bytes 786440 | tf_op jit(solution)/shard_map/ppermute | solution.py:466
  8.4 35.0 %copy-start = (bf16[7,2,256,256]{3,2,1,0:T(8,128)(2,1)S(1)}, bf16[7,2,256,256]{3,2,1,0:T(8,128)(2,1)}, u32[]{:S(2)}) copy-start(bf16[7,2,256,256]{3,2,1,0:T(8,128)(2,1)} %elems.1) | copy-start | bytes 5505028
  8.4 35.0 %copy-start.1 = (s32[1,2,2]{2,1,0:T(2,128)S(1)}, s32[1,2,2]{2,1,0:T(2,128)}, u32[]{:S(2)}) copy-start(s32[1,2,2]{2,1,0:T(2,128)} %diag_mom.1) | copy-start | bytes 52
  8.4 29.0 %collective-permute-start.4 = (bf16[2,128,512]{2,1,0:T(8,128)(2,1)S(1)}, bf16[2,128,512]{2,1,0:T(8,128)(2,1)S(1)}, u32[]{:S(2)}, u32[]{:S(2)}) collective-permute-start(bf16[2,128,512]{2,1,0:T(8,128)(2,1)S(1)} %get-tuple-element.33), channel_id=1, source_target_pairs={{0,14},{1,15},{2,12},{3,13},{4,10},{5,11},{6,8},{7,9},{8,2},{9,3},... | collective-permute-start | bytes 786440 | tf_op jit(solution)/shard_map/ppermute | solution.py:466
  20.6 22.9 %collective-permute-start.5 = (bf16[2,128,512]{2,1,0:T(8,128)(2,1)S(1)}, bf16[2,128,512]{2,1,0:T(8,128)(2,1)S(1)}, u32[]{:S(2)}, u32[]{:S(2)}) collective-permute-start(bf16[2,128,512]{2,1,0:T(8,128)(2,1)S(1)} %get-tuple-element.34), channel_id=1, source_target_pairs={{0,2},{1,3},{2,0},{3,1},{4,6},{5,7},{6,4},{7,5},{8,10},{9,11},{10,... | collective-permute-start | bytes 786440 | tf_op jit(solution)/shard_map/ppermute | solution.py:466
  26.2 18.2 %collective-permute-start.6 = (bf16[2,128,512]{2,1,0:T(8,128)(2,1)S(1)}, bf16[2,128,512]{2,1,0:T(8,128)(2,1)S(1)}, u32[]{:S(2)}, u32[]{:S(2)}) collective-permute-start(bf16[2,128,512]{2,1,0:T(8,128)(2,1)S(1)} %get-tuple-element.35), channel_id=1, source_target_pairs={{0,1},{1,0},{2,3},{3,2},{4,5},{5,4},{6,7},{7,6},{8,9},{9,8},{10,11... | collective-permute-start | bytes 786440 | tf_op jit(solution)/shard_map/ppermute | solution.py:466
  29.0 16.4 %collective-permute-start.7 = (bf16[2,128,512]{2,1,0:T(8,128)(2,1)S(1)}, bf16[2,128,512]{2,1,0:T(8,128)(2,1)S(1)}, u32[]{:S(2)}, u32[]{:S(2)}) collective-permute-start(bf16[2,128,512]{2,1,0:T(8,128)(2,1)S(1)} %get-tuple-element.36), channel_id=1, source_target_pairs={{0,4},{1,5},{2,6},{3,7},{4,0},{5,1},{6,2},{7,3},{8,12},{9,13},{10,... | collective-permute-start | bytes 786440 | tf_op jit(solution)/shard_map/ppermute | solution.py:466
  33.2 15.8 %collective-permute-start.8 = (bf16[2,128,512]{2,1,0:T(8,128)(2,1)S(1)}, bf16[2,128,512]{2,1,0:T(8,128)(2,1)S(1)}, u32[]{:S(2)}, u32[]{:S(2)}) collective-permute-start(bf16[2,128,512]{2,1,0:T(8,128)(2,1)S(1)} %get-tuple-element.37), channel_id=1, source_target_pairs={{0,15},{1,14},{2,13},{3,12},{4,11},{5,10},{6,9},{7,8},{8,3},{9,2},... | collective-permute-start | bytes 786440 | tf_op jit(solution)/shard_map/ppermute | solution.py:466
  37.4 16.4 %collective-permute-start.9 = (bf16[2,128,512]{2,1,0:T(8,128)(2,1)S(1)}, bf16[2,128,512]{2,1,0:T(8,128)(2,1)S(1)}, u32[]{:S(2)}, u32[]{:S(2)}) collective-permute-start(bf16[2,128,512]{2,1,0:T(8,128)(2,1)S(1)} %get-tuple-element.38), channel_id=1, source_target_pairs={{0,3},{1,2},{2,1},{3,0},{4,7},{5,6},{6,5},{7,4},{8,11},{9,10},{10,... | collective-permute-start | bytes 786440 | tf_op jit(solution)/shard_map/ppermute | solution.py:466
  43.4 12.7 %collective-permute-start.10 = (bf16[2,128,512]{2,1,0:T(8,128)(2,1)S(1)}, bf16[2,128,512]{2,1,0:T(8,128)(2,1)S(1)}, u32[]{:S(2)}, u32[]{:S(2)}) collective-permute-start(bf16[2,128,512]{2,1,0:T(8,128)(2,1)S(1)} %get-tuple-element.39), channel_id=1, source_target_pairs={{0,5},{1,4},{2,7},{3,6},{4,1},{5,0},{6,3},{7,2},{8,13},{9,12},{10,... | collective-permute-start | bytes 786440 | tf_op jit(solution)/shard_map/ppermute | solution.py:466
  44.4 45.9 %collective-permute-start.11 = (bf16[2,128,512]{2,1,0:T(8,128)(2,1)S(1)}, bf16[2,128,512]{2,1,0:T(8,128)(2,1)S(1)}, u32[]{:S(2)}, u32[]{:S(2)}) collective-permute-start(bf16[2,128,512]{2,1,0:T(8,128)(2,1)S(1)} %get-tuple-element.46), channel_id=1, source_target_pairs={{0,8},{1,9},{2,10},{3,11},{4,12},{5,13},{6,14},{7,15},{8,4},{9,5},... | collective-permute-start | bytes 786440 | tf_op jit(solution)/shard_map/ppermute | solution.py:466
  45.4 44.9 %collective-permute-start.12 = (bf16[2,128,512]{2,1,0:T(8,128)(2,1)S(1)}, bf16[2,128,512]{2,1,0:T(8,128)(2,1)S(1)}, u32[]{:S(2)}, u32[]{:S(2)}) collective-permute-start(bf16[2,128,512]{2,1,0:T(8,128)(2,1)S(1)} %get-tuple-element.47), channel_id=1, source_target_pairs={{0,10},{1,11},{2,8},{3,9},{4,14},{5,15},{6,12},{7,13},{8,6},{9,7},... | collective-permute-start | bytes 786440 | tf_op jit(solution)/shard_map/ppermute | solution.py:466
  49.0 42.7 %collective-permute-start.13 = (bf16[2,128,512]{2,1,0:T(8,128)(2,1)S(1)}, bf16[2,128,512]{2,1,0:T(8,128)(2,1)S(1)}, u32[]{:S(2)}, u32[]{:S(2)}) collective-permute-start(bf16[2,128,512]{2,1,0:T(8,128)(2,1)S(1)} %get-tuple-element.48), channel_id=1, source_target_pairs={{0,9},{1,8},{2,11},{3,10},{4,13},{5,12},{6,15},{7,14},{8,5},{9,4},... | collective-permute-start | bytes 786440 | tf_op jit(solution)/shard_map/ppermute | solution.py:466
  53.8 42.6 %collective-permute-start.14 = (bf16[2,128,512]{2,1,0:T(8,128)(2,1)S(1)}, bf16[2,128,512]{2,1,0:T(8,128)(2,1)S(1)}, u32[]{:S(2)}, u32[]{:S(2)}) collective-permute-start(bf16[2,128,512]{2,1,0:T(8,128)(2,1)S(1)} %get-tuple-element.49), channel_id=1, source_target_pairs={{0,11},{1,10},{2,9},{3,8},{4,15},{5,14},{6,13},{7,12},{8,7},{9,6},... | collective-permute-start | bytes 786440 | tf_op jit(solution)/shard_map/ppermute | solution.py:466
  97.1 2.0 %collective-permute-start.16 = (bf16[2,2,256,256]{3,2,1,0:T(8,128)(2,1)S(1)}, bf16[2,2,256,256]{3,2,1,0:T(8,128)(2,1)S(1)}, u32[]{:S(2)}, u32[]{:S(2)}) collective-permute-start(bf16[2,2,256,256]{3,2,1,0:T(8,128)(2,1)S(1)} %get-tuple-element.52.own), channel_id=1, source_target_pairs={{0,1},{1,0},{2,3},{3,2},{4,5},{5,4},{6,7},{7,6},{8,9},{9,8},{10,11... | collective-permute-start | bytes 1572872 | tf_op jit(solution)/shard_map/ppermute | solution.py:480
  98.0 2.4 %collective-permute-start.15 = (bf16[2,2,256,256]{3,2,1,0:T(8,128)(2,1)S(1)}, bf16[2,2,256,256]{3,2,1,0:T(8,128)(2,1)S(1)}, u32[]{:S(2)}, u32[]{:S(2)}) collective-permute-start(bf16[2,2,256,256]{3,2,1,0:T(8,128)(2,1)S(1)} %late_rest.1.rest.own), channel_id=1, source_target_pairs={{0,1},{1,0},{2,3},{3,2},{4,5},{5,4},{6,7},{7,6},{8,9},{9,8},{10,11... | collective-permute-start | bytes 1572872 | tf_op jit(solution)/shard_map/ppermute | solution.py:482
  101.4 1.3 %collective-permute-start.17 = (f32[6,8,128]{2,1,0:T(8,128)S(1)}, f32[6,8,128]{2,1,0:T(8,128)S(1)}, u32[]{:S(2)}, u32[]{:S(2)}) collective-permute-start(f32[6,8,128]{2,1,0:T(8,128)S(1)} %last_cross.1.mine), channel_id=1, source_target_pairs={{0,1},{1,0},{2,3},{3,2},{4,5},{5,4},{6,7},{7,6},{8,9},{9,8},{10,11... | collective-permute-start | bytes 73736 | tf_op jit(solution)/shard_map/ppermute | solution.py:486
